TPU v7x, 128 devices: a whole 4x4x4 slice. The times are simulated.
128 devices in a mesh: section: 8 (over z, core), ctx: 16 (over x, y).
Axes of the slice: x: 4, y: 4, z: 4, core: 2. Of those that a mesh axis runs over, the one named last changes fastest.
Arguments:
- embedded: bfloat16 [4096, 2560], P('ctx')
- finished: bfloat16 [8, 4096, 2560], P('section', 'ctx')
- norm_gain: float32 [8, 2560], P('section'), may hold values from 0.5 to 1.5
- q_weight: bfloat16 [8, 2560, 2560], P('section')
- kv_weight: bfloat16 [8, 2560, 1024], P('section')
- out_gain: float32 [8, 2560], P('section'), may hold values from 0.5 to 1.5
- span_order: int32 [16], replicated, may hold values from 0 to 15, each once
Outputs:
- layer_out: bfloat16 [8, 4096, 2560], P('section', 'ctx')
Inputs may be any that keep to these rules, and one draw needn't show every extreme that they name: `span_order`: each ctx index holds a different span.
All inputs are finite; a program needn't handle non-finite values. Where the computation divides by a largest or mean magnitude, that divisor is 1e-20 or more.
Results may differ from a plain program's by a relative error of at most 0.0095.
Values may be sent and summed in bfloat16 or wider, within the bound.
A program may use at most 128 MiB of HBM per device.

v0:
```python
import math

import jax
import jax.numpy as jnp
from jax import lax
from jax.sharding import PartitionSpec as P

QUERY_HEADS = 20
KEY_VALUE_HEADS = 4
HEAD_DIM = 128
QBLOCK = 128


EPSILON = 1e-06
MASK_FILLER = -1e30


def shifted(x, axis, by):
    count = lax.axis_size(axis)
    pairs = [(i, i + by) for i in range(count) if 0 <= i + by < count]
    return lax.ppermute(x, axis, pairs)


def normalize(vector, gain_row):
    return (
        vector * lax.rsqrt(jnp.mean(vector * vector, axis=-1, keepdims=True) + EPSILON) * gain_row
    )


def block_scaled(hidden_rows):
    count_of_rows, model_width = hidden_rows.shape
    grouped = hidden_rows.astype(jnp.float32).reshape(count_of_rows, model_width // QBLOCK, QBLOCK)
    scale_bf = (jnp.max(jnp.abs(grouped), axis=-1) + EPSILON).astype(jnp.bfloat16)
    coded_rows = (grouped / scale_bf.astype(jnp.float32)[..., None]).astype(jnp.bfloat16)
    return (coded_rows, scale_bf)


def per_device(embedded, finished, norm_gain, q_weight, kv_weight, out_gain, span_order):
    count_of_rows, model_width = embedded.shape
    group_width = QUERY_HEADS // KEY_VALUE_HEADS
    inv_root = HEAD_DIM ** (-0.5)
    ctx_index = lax.axis_index("ctx")
    coded_rows, block_scales = block_scaled(finished[0])
    coded_rows, block_scales = shifted((coded_rows, block_scales), "section", 1)
    arrived = (
        coded_rows.astype(jnp.float32) * block_scales.astype(jnp.float32)[..., None]
    ).reshape(count_of_rows, model_width)
    hidden_in = jnp.where(lax.axis_index("section") == 0, embedded.astype(jnp.float32), arrived)
    normed = normalize(hidden_in, norm_gain[0]).astype(jnp.bfloat16)
    query_matrix = jnp.dot(normed, q_weight[0], preferred_element_type=jnp.float32).astype(
        jnp.bfloat16
    )
    own_order = lax.dynamic_slice_in_dim(span_order, ctx_index, 1)[0]
    query_order = jnp.full((count_of_rows,), own_order, jnp.int32)
    query_row = jnp.arange(count_of_rows)
    query_matrix = query_matrix.reshape(count_of_rows, KEY_VALUE_HEADS, group_width, HEAD_DIM)

    def scores_step(state_now, key_block):
        key_value_rows, key_order, key_row = key_block
        block_length = key_value_rows.shape[0]
        key_portion = key_value_rows[:, : KEY_VALUE_HEADS * HEAD_DIM].reshape(
            block_length, KEY_VALUE_HEADS, HEAD_DIM
        )
        value_portion = key_value_rows[:, KEY_VALUE_HEADS * HEAD_DIM :].reshape(
            block_length, KEY_VALUE_HEADS, HEAD_DIM
        )
        peak_now, totals, accumulated = state_now
        scores = (
            jnp.einsum(
                "rkgd,skd->kgrs", query_matrix, key_portion, preferred_element_type=jnp.float32
            )
            * inv_root
        )
        visible = (key_order[None, :] < query_order[:, None]) | (
            key_order[None, :] == query_order[:, None]
        ) & (key_row[None, :] <= query_row[:, None])
        scores = jnp.where(visible, scores, MASK_FILLER)
        peak_next = jnp.maximum(peak_now, jnp.max(scores, axis=-1))
        weights = jnp.where(visible, jnp.exp(scores - peak_next[..., None]), 0.0)
        rescale = jnp.exp(peak_now - peak_next)
        totals = totals * rescale + jnp.sum(weights, axis=-1)
        accumulated = accumulated * rescale[..., None] + jnp.einsum(
            "kgrs,skd->kgrd",
            weights.astype(jnp.bfloat16),
            value_portion,
            preferred_element_type=jnp.float32,
        )
        return (peak_next, totals, accumulated)

    def visit(state_now, key_block):
        state_next = scores_step(state_now, key_block)
        return (state_next, None)

    initial = (
        jnp.full((KEY_VALUE_HEADS, group_width, count_of_rows), MASK_FILLER, jnp.float32),
        jnp.zeros((KEY_VALUE_HEADS, group_width, count_of_rows), jnp.float32),
        jnp.zeros((KEY_VALUE_HEADS, group_width, count_of_rows, HEAD_DIM), jnp.float32),
    )
    key_value_pair = jnp.dot(normed, kv_weight[0], preferred_element_type=jnp.float32).astype(
        jnp.bfloat16
    )
    key_value_rows = lax.all_gather(key_value_pair, "ctx", axis=0, tiled=True)
    total_rows = key_value_rows.shape[0]
    key_order = jnp.repeat(span_order, count_of_rows)
    key_row = jnp.arange(total_rows) % count_of_rows
    block_length = math.gcd(total_rows, 512)
    block_count = total_rows // block_length
    blocks = (
        key_value_rows.reshape(block_count, block_length, key_value_rows.shape[1]),
        key_order.reshape(block_count, block_length),
        key_row.reshape(block_count, block_length),
    )
    state_next, unused = lax.scan(visit, initial, blocks)
    peak_last, totals, accumulated = state_next
    attended = (
        (accumulated / totals[..., None]).transpose(2, 0, 1, 3).reshape(count_of_rows, model_width)
    )
    output_rows = hidden_in + out_gain[0] * normalize(attended, 1.0)
    return output_rows.astype(jnp.bfloat16)[None]


def solution(mesh):
    placed = (
        P("ctx", None),
        P("section", "ctx", None),
        P("section", None),
        P("section", None, None),
        P("section", None, None),
        P("section", None),
        P(),
    )
    return jax.shard_map(
        per_device, mesh=mesh, in_specs=placed, out_specs=P("section", "ctx", None), check_vma=False
    )
```

profile of v0, /device:TPU:106, one launch (start us, length us, event | category | flops | bytes accessed | tf_op | source)
XLA Modules:
  0.0 304.8 jit_solution(10125124778029962290)
XLA Ops:
  6.5 1.6 copy.16
  8.7 1.9 collective-permute-start
  10.7 1.9 collective-permute-start.1
  12.6 1.6 copy.15
  14.3 13.5 %collective-permute-done.1 = bf16[256,20]{0,1:T(8,128)(2,1)S(1)} collective-permute-done((bf16[256,20]{0,1:T(8,128)(2,1)S(1)}, bf16[256,20]{0,1:T(8,128)(2,1)S(1)}, u32[]{:S(2)}, u32[]{:S(2)}) %collective-permute-start.1) | collective-permute-done | bytes 10272 | tf_op jit(solution)/shard_map/ppermute | solution.py:21
  27.8 1.8 convert_multiply_fusion
  31.8 2.4 fusion.32
  35.7 8.3 %fusion.23 = bf16[256,2560]{1,0:T(8,128)(2,1)S(1)} fusion(bf16[256,2560]{0,1:T(8,128)(2,1)S(1)} %multiply_convert_fusion, bf16[1,2560,2560]{2,1,0:T(8,128)(2,1)} %param.12), kind=kOutput, calls=%fused_computation.30 | convolution fusion | flops 3356098560 | bytes 15728640 | tf_op jit(solution)/shard_map/dot_general | solution.py:50
  44.6 0.8 copy.20
  45.4 59.5 %all-gather.2.cloned.1.call-done = bf16[4096,1024]{1,0:T(8,128)(2,1)} async-done(((bf16[256,1024]{1,0:T(8,128)(2,1)}), bf16[4096,1024]{1,0:T(8,128)(2,1)}) %all-gather.2.cloned.1.call-update) | async-done | bytes 8388624 | tf_op jit(solution)/shard_map/all_gather | solution.py:102
  105.5 186.0 %while.15 = (s32[]{:T(128)}, f32[4,5,256]{2,1,0:T(8,128)}, f32[4,5,256]{2,1,0:T(8,128)}, f32[4,5,256,128]{3,2,1,0:T(8,128)}, s32[8,512]{1,0:T(8,128)}, /*index=5...) while((s32[]{:T(128)}, f32[4,5,256]{2,1,0:T(8,128)}, ...), condition=%wide.region_5.6_spmd.clone, body=%wide.region_2.5_spmd.clone.sunk | while | flops 1378641920 | bytes 88406256 | solution.py:113
  107.2 1.3 constant_dynamic-slice_fusion.6
  109.2 5.8 %fusion.59 = (f32[4,5,256]{2,1,0:T(8,128)S(1)}, f32[4,512,256,5]{2,1,3,0:T(8,128)}) fusion(pred[256,512]{0,1:T(8,128)(4,1)S(1)} %fusion.57, bf16[512,4,128,1]{0,2,3,1:T(8,128)(2,1)S(1)} %bitcast.92, bf16[256,4,5,128]{3,0,2,1:T(8,128)(2,1)S(1)} %get-tuple-element.249), kind=kOutput, calls=%fused_computation.4.clone.1 | convolution fusion | flops 678947840 | bytes 12472320 | tf_op jit(solution)/shard_map/while/body/eval_jaxpr/rkgd,skd->kgrs/dot_general | solution.py:69
  115.0 6.7 %fusion.60 = f32[4,5,256]{2,1,0:T(8,128)S(1)} fusion(f32[4,512,256,5]{2,1,3,0:T(8,128)} %get-tuple-element.216, f32[4,5,256]{2,1,0:T(8,128)S(1)} %select_maximum_fusion.2, pred[256,512]{0,1:T(8,128)(4,1)S(1)} %fusion.57), kind=kLoop, calls=%fused_computation.6.clone.1 | loop fusion | flops 13102080 | bytes 10657792 | tf_op jit(solution)/shard_map/while/body/eval_jaxpr/reduce_sum | solution.py:81
  122.0 4.9 %fusion.62 = f32[4,5,256,128]{3,2,1,0:T(8,128)} fusion(f32[4,5,256,128]{3,2,1,0:T(8,128)} %get-tuple-element.234, bf16[512,4,128,1]{0,2,3,1:T(8,128)(2,1)S(1)} %bitcast.93, f32[4,512,256,5]{2,1,3,0:T(8,128)S(1)} %copy-done, f32[4,5,256]{2,1,0:T(8,128)S(1)} %select_maximum_fusion.2, pred[256,512]{0,1:T(8,128)(4,1)S(1)} %fusion.57, ...), kind=kOutput, calls=%fused_computation.10.clone.1 | convolution fusion | flops 686161920 | bytes 16424961 | tf_op jit(solution)/shard_map/while/body/eval_jaxpr/kgrs,skd->kgrd/dot_general | solution.py:82
  129.2 1.3 constant_dynamic-slice_fusion.6
  131.2 5.8 %fusion.59 = (f32[4,5,256]{2,1,0:T(8,128)S(1)}, f32[4,512,256,5]{2,1,3,0:T(8,128)}) fusion(pred[256,512]{0,1:T(8,128)(4,1)S(1)} %fusion.57, bf16[512,4,128,1]{0,2,3,1:T(8,128)(2,1)S(1)} %bitcast.92, bf16[256,4,5,128]{3,0,2,1:T(8,128)(2,1)S(1)} %get-tuple-element.249), kind=kOutput, calls=%fused_computation.4.clone.1 | convolution fusion | flops 678947840 | bytes 12472320 | tf_op jit(solution)/shard_map/while/body/eval_jaxpr/rkgd,skd->kgrs/dot_general | solution.py:69
  137.0 6.7 %fusion.60 = f32[4,5,256]{2,1,0:T(8,128)S(1)} fusion(f32[4,512,256,5]{2,1,3,0:T(8,128)} %get-tuple-element.216, f32[4,5,256]{2,1,0:T(8,128)S(1)} %select_maximum_fusion.2, pred[256,512]{0,1:T(8,128)(4,1)S(1)} %fusion.57), kind=kLoop, calls=%fused_computation.6.clone.1 | loop fusion | flops 13102080 | bytes 10657792 | tf_op jit(solution)/shard_map/while/body/eval_jaxpr/reduce_sum | solution.py:81
  144.0 6.3 %fusion.62 = f32[4,5,256,128]{3,2,1,0:T(8,128)} fusion(f32[4,5,256,128]{3,2,1,0:T(8,128)} %get-tuple-element.234, bf16[512,4,128,1]{0,2,3,1:T(8,128)(2,1)S(1)} %bitcast.93, f32[4,512,256,5]{2,1,3,0:T(8,128)S(1)} %copy-done, f32[4,5,256]{2,1,0:T(8,128)S(1)} %select_maximum_fusion.2, pred[256,512]{0,1:T(8,128)(4,1)S(1)} %fusion.57, ...), kind=kOutput, calls=%fused_computation.10.clone.1 | convolution fusion | flops 686161920 | bytes 16424961 | tf_op jit(solution)/shard_map/while/body/eval_jaxpr/kgrs,skd->kgrd/dot_general | solution.py:82
  150.9 0.7 constant_dynamic-slice_fusion.5
  152.6 1.3 constant_dynamic-slice_fusion.6
  154.6 5.8 %fusion.59 = (f32[4,5,256]{2,1,0:T(8,128)S(1)}, f32[4,512,256,5]{2,1,3,0:T(8,128)}) fusion(pred[256,512]{0,1:T(8,128)(4,1)S(1)} %fusion.57, bf16[512,4,128,1]{0,2,3,1:T(8,128)(2,1)S(1)} %bitcast.92, bf16[256,4,5,128]{3,0,2,1:T(8,128)(2,1)S(1)} %get-tuple-element.249), kind=kOutput, calls=%fused_computation.4.clone.1 | convolution fusion | flops 678947840 | bytes 12472320 | tf_op jit(solution)/shard_map/while/body/eval_jaxpr/rkgd,skd->kgrs/dot_general | solution.py:69
  160.5 6.7 %fusion.60 = f32[4,5,256]{2,1,0:T(8,128)S(1)} fusion(f32[4,512,256,5]{2,1,3,0:T(8,128)} %get-tuple-element.216, f32[4,5,256]{2,1,0:T(8,128)S(1)} %select_maximum_fusion.2, pred[256,512]{0,1:T(8,128)(4,1)S(1)} %fusion.57), kind=kLoop, calls=%fused_computation.6.clone.1 | loop fusion | flops 13102080 | bytes 10657792 | tf_op jit(solution)/shard_map/while/body/eval_jaxpr/reduce_sum | solution.py:81
  167.4 6.3 %fusion.62 = f32[4,5,256,128]{3,2,1,0:T(8,128)} fusion(f32[4,5,256,128]{3,2,1,0:T(8,128)} %get-tuple-element.234, bf16[512,4,128,1]{0,2,3,1:T(8,128)(2,1)S(1)} %bitcast.93, f32[4,512,256,5]{2,1,3,0:T(8,128)S(1)} %copy-done, f32[4,5,256]{2,1,0:T(8,128)S(1)} %select_maximum_fusion.2, pred[256,512]{0,1:T(8,128)(4,1)S(1)} %fusion.57, ...), kind=kOutput, calls=%fused_computation.10.clone.1 | convolution fusion | flops 686161920 | bytes 16424961 | tf_op jit(solution)/shard_map/while/body/eval_jaxpr/kgrs,skd->kgrd/dot_general | solution.py:82
  174.4 0.7 constant_dynamic-slice_fusion.5
  176.1 1.3 constant_dynamic-slice_fusion.6
  178.0 5.8 %fusion.59 = (f32[4,5,256]{2,1,0:T(8,128)S(1)}, f32[4,512,256,5]{2,1,3,0:T(8,128)}) fusion(pred[256,512]{0,1:T(8,128)(4,1)S(1)} %fusion.57, bf16[512,4,128,1]{0,2,3,1:T(8,128)(2,1)S(1)} %bitcast.92, bf16[256,4,5,128]{3,0,2,1:T(8,128)(2,1)S(1)} %get-tuple-element.249), kind=kOutput, calls=%fused_computation.4.clone.1 | convolution fusion | flops 678947840 | bytes 12472320 | tf_op jit(solution)/shard_map/while/body/eval_jaxpr/rkgd,skd->kgrs/dot_general | solution.py:69
  183.9 6.7 %fusion.60 = f32[4,5,256]{2,1,0:T(8,128)S(1)} fusion(f32[4,512,256,5]{2,1,3,0:T(8,128)} %get-tuple-element.216, f32[4,5,256]{2,1,0:T(8,128)S(1)} %select_maximum_fusion.2, pred[256,512]{0,1:T(8,128)(4,1)S(1)} %fusion.57), kind=kLoop, calls=%fused_computation.6.clone.1 | loop fusion | flops 13102080 | bytes 10657792 | tf_op jit(solution)/shard_map/while/body/eval_jaxpr/reduce_sum | solution.py:81
  190.9 6.3 %fusion.62 = f32[4,5,256,128]{3,2,1,0:T(8,128)} fusion(f32[4,5,256,128]{3,2,1,0:T(8,128)} %get-tuple-element.234, bf16[512,4,128,1]{0,2,3,1:T(8,128)(2,1)S(1)} %bitcast.93, f32[4,512,256,5]{2,1,3,0:T(8,128)S(1)} %copy-done, f32[4,5,256]{2,1,0:T(8,128)S(1)} %select_maximum_fusion.2, pred[256,512]{0,1:T(8,128)(4,1)S(1)} %fusion.57, ...), kind=kOutput, calls=%fused_computation.10.clone.1 | convolution fusion | flops 686161920 | bytes 16424961 | tf_op jit(solution)/shard_map/while/body/eval_jaxpr/kgrs,skd->kgrd/dot_general | solution.py:82
  199.5 1.3 constant_dynamic-slice_fusion.6
  201.4 5.8 %fusion.59 = (f32[4,5,256]{2,1,0:T(8,128)S(1)}, f32[4,512,256,5]{2,1,3,0:T(8,128)}) fusion(pred[256,512]{0,1:T(8,128)(4,1)S(1)} %fusion.57, bf16[512,4,128,1]{0,2,3,1:T(8,128)(2,1)S(1)} %bitcast.92, bf16[256,4,5,128]{3,0,2,1:T(8,128)(2,1)S(1)} %get-tuple-element.249), kind=kOutput, calls=%fused_computation.4.clone.1 | convolution fusion | flops 678947840 | bytes 12472320 | tf_op jit(solution)/shard_map/while/body/eval_jaxpr/rkgd,skd->kgrs/dot_general | solution.py:69
  207.3 6.7 %fusion.60 = f32[4,5,256]{2,1,0:T(8,128)S(1)} fusion(f32[4,512,256,5]{2,1,3,0:T(8,128)} %get-tuple-element.216, f32[4,5,256]{2,1,0:T(8,128)S(1)} %select_maximum_fusion.2, pred[256,512]{0,1:T(8,128)(4,1)S(1)} %fusion.57), kind=kLoop, calls=%fused_computation.6.clone.1 | loop fusion | flops 13102080 | bytes 10657792 | tf_op jit(solution)/shard_map/while/body/eval_jaxpr/reduce_sum | solution.py:81
  214.3 6.3 %fusion.62 = f32[4,5,256,128]{3,2,1,0:T(8,128)} fusion(f32[4,5,256,128]{3,2,1,0:T(8,128)} %get-tuple-element.234, bf16[512,4,128,1]{0,2,3,1:T(8,128)(2,1)S(1)} %bitcast.93, f32[4,512,256,5]{2,1,3,0:T(8,128)S(1)} %copy-done, f32[4,5,256]{2,1,0:T(8,128)S(1)} %select_maximum_fusion.2, pred[256,512]{0,1:T(8,128)(4,1)S(1)} %fusion.57, ...), kind=kOutput, calls=%fused_computation.10.clone.1 | convolution fusion | flops 686161920 | bytes 16424961 | tf_op jit(solution)/shard_map/while/body/eval_jaxpr/kgrs,skd->kgrd/dot_general | solution.py:82
  222.9 1.3 constant_dynamic-slice_fusion.6
  224.9 5.8 %fusion.59 = (f32[4,5,256]{2,1,0:T(8,128)S(1)}, f32[4,512,256,5]{2,1,3,0:T(8,128)}) fusion(pred[256,512]{0,1:T(8,128)(4,1)S(1)} %fusion.57, bf16[512,4,128,1]{0,2,3,1:T(8,128)(2,1)S(1)} %bitcast.92, bf16[256,4,5,128]{3,0,2,1:T(8,128)(2,1)S(1)} %get-tuple-element.249), kind=kOutput, calls=%fused_computation.4.clone.1 | convolution fusion | flops 678947840 | bytes 12472320 | tf_op jit(solution)/shard_map/while/body/eval_jaxpr/rkgd,skd->kgrs/dot_general | solution.py:69
  230.7 6.7 %fusion.60 = f32[4,5,256]{2,1,0:T(8,128)S(1)} fusion(f32[4,512,256,5]{2,1,3,0:T(8,128)} %get-tuple-element.216, f32[4,5,256]{2,1,0:T(8,128)S(1)} %select_maximum_fusion.2, pred[256,512]{0,1:T(8,128)(4,1)S(1)} %fusion.57), kind=kLoop, calls=%fused_computation.6.clone.1 | loop fusion | flops 13102080 | bytes 10657792 | tf_op jit(solution)/shard_map/while/body/eval_jaxpr/reduce_sum | solution.py:81
  237.7 6.3 %fusion.62 = f32[4,5,256,128]{3,2,1,0:T(8,128)} fusion(f32[4,5,256,128]{3,2,1,0:T(8,128)} %get-tuple-element.234, bf16[512,4,128,1]{0,2,3,1:T(8,128)(2,1)S(1)} %bitcast.93, f32[4,512,256,5]{2,1,3,0:T(8,128)S(1)} %copy-done, f32[4,5,256]{2,1,0:T(8,128)S(1)} %select_maximum_fusion.2, pred[256,512]{0,1:T(8,128)(4,1)S(1)} %fusion.57, ...), kind=kOutput, calls=%fused_computation.10.clone.1 | convolution fusion | flops 686161920 | bytes 16424961 | tf_op jit(solution)/shard_map/while/body/eval_jaxpr/kgrs,skd->kgrd/dot_general | solution.py:82
  246.4 1.3 constant_dynamic-slice_fusion.6
  248.3 5.8 %fusion.59 = (f32[4,5,256]{2,1,0:T(8,128)S(1)}, f32[4,512,256,5]{2,1,3,0:T(8,128)}) fusion(pred[256,512]{0,1:T(8,128)(4,1)S(1)} %fusion.57, bf16[512,4,128,1]{0,2,3,1:T(8,128)(2,1)S(1)} %bitcast.92, bf16[256,4,5,128]{3,0,2,1:T(8,128)(2,1)S(1)} %get-tuple-element.249), kind=kOutput, calls=%fused_computation.4.clone.1 | convolution fusion | flops 678947840 | bytes 12472320 | tf_op jit(solution)/shard_map/while/body/eval_jaxpr/rkgd,skd->kgrs/dot_general | solution.py:69
  254.2 6.7 %fusion.60 = f32[4,5,256]{2,1,0:T(8,128)S(1)} fusion(f32[4,512,256,5]{2,1,3,0:T(8,128)} %get-tuple-element.216, f32[4,5,256]{2,1,0:T(8,128)S(1)} %select_maximum_fusion.2, pred[256,512]{0,1:T(8,128)(4,1)S(1)} %fusion.57), kind=kLoop, calls=%fused_computation.6.clone.1 | loop fusion | flops 13102080 | bytes 10657792 | tf_op jit(solution)/shard_map/while/body/eval_jaxpr/reduce_sum | solution.py:81
  261.1 6.3 %fusion.62 = f32[4,5,256,128]{3,2,1,0:T(8,128)} fusion(f32[4,5,256,128]{3,2,1,0:T(8,128)} %get-tuple-element.234, bf16[512,4,128,1]{0,2,3,1:T(8,128)(2,1)S(1)} %bitcast.93, f32[4,512,256,5]{2,1,3,0:T(8,128)S(1)} %copy-done, f32[4,5,256]{2,1,0:T(8,128)S(1)} %select_maximum_fusion.2, pred[256,512]{0,1:T(8,128)(4,1)S(1)} %fusion.57, ...), kind=kOutput, calls=%fused_computation.10.clone.1 | convolution fusion | flops 686161920 | bytes 16424961 | tf_op jit(solution)/shard_map/while/body/eval_jaxpr/kgrs,skd->kgrd/dot_general | solution.py:82
  269.8 1.3 constant_dynamic-slice_fusion.6
  271.7 5.8 %fusion.59 = (f32[4,5,256]{2,1,0:T(8,128)S(1)}, f32[4,512,256,5]{2,1,3,0:T(8,128)}) fusion(pred[256,512]{0,1:T(8,128)(4,1)S(1)} %fusion.57, bf16[512,4,128,1]{0,2,3,1:T(8,128)(2,1)S(1)} %bitcast.92, bf16[256,4,5,128]{3,0,2,1:T(8,128)(2,1)S(1)} %get-tuple-element.249), kind=kOutput, calls=%fused_computation.4.clone.1 | convolution fusion | flops 678947840 | bytes 12472320 | tf_op jit(solution)/shard_map/while/body/eval_jaxpr/rkgd,skd->kgrs/dot_general | solution.py:69
  277.6 6.7 %fusion.60 = f32[4,5,256]{2,1,0:T(8,128)S(1)} fusion(f32[4,512,256,5]{2,1,3,0:T(8,128)} %get-tuple-element.216, f32[4,5,256]{2,1,0:T(8,128)S(1)} %select_maximum_fusion.2, pred[256,512]{0,1:T(8,128)(4,1)S(1)} %fusion.57), kind=kLoop, calls=%fused_computation.6.clone.1 | loop fusion | flops 13102080 | bytes 10657792 | tf_op jit(solution)/shard_map/while/body/eval_jaxpr/reduce_sum | solution.py:81
  284.6 6.3 %fusion.62 = f32[4,5,256,128]{3,2,1,0:T(8,128)} fusion(f32[4,5,256,128]{3,2,1,0:T(8,128)} %get-tuple-element.234, bf16[512,4,128,1]{0,2,3,1:T(8,128)(2,1)S(1)} %bitcast.93, f32[4,512,256,5]{2,1,3,0:T(8,128)S(1)} %copy-done, f32[4,5,256]{2,1,0:T(8,128)S(1)} %select_maximum_fusion.2, pred[256,512]{0,1:T(8,128)(4,1)S(1)} %fusion.57, ...), kind=kOutput, calls=%fused_computation.10.clone.1 | convolution fusion | flops 686161920 | bytes 16424961 | tf_op jit(solution)/shard_map/while/body/eval_jaxpr/kgrs,skd->kgrd/dot_general | solution.py:82
  291.5 2.2 copy.21
  294.2 1.2 copy-done.2
  296.3 1.6 copy.22
  (170 shorter events, 31.3 us)
Async XLA Ops:
  6.5 98.3 %all-gather.2.cloned.1.call-start = ((), (), s32[]{:S(2)}) async-start(), calls=%async_computation | async-start | bytes 8912896 | tf_op jit(solution)/shard_map/all_gather | solution.py:102
  8.4 5.8 %copy-start.9 = (f32[1,2560]{1,0:T(1,128)S(1)}, f32[1,2560]{1,0:T(1,128)}, u32[]{:S(2)}) copy-start(f32[1,2560]{1,0:T(1,128)} %param.11) | copy-start | bytes 30724
  8.7 19.1 %collective-permute-start = (bf16[256,20,128]{0,2,1:T(8,128)(2,1)S(1)}, bf16[256,20,128]{0,2,1:T(8,128)(2,1)}, u32[]{:S(2)}, u32[]{:S(2)}) collective-permute-start(bf16[256,20,128]{0,2,1:T(8,128)(2,1)S(1)} %fusion.27), channel_id=1, source_target_pairs={{0,16},{16,32},{32,48},{48,64},{64,80},{80,96},{96,112},{1,17},{17... | collective-permute-start | bytes 3932168 | tf_op jit(solution)/shard_map/ppermute | solution.py:21
  10.7 17.1 %collective-permute-start.1 = (bf16[256,20]{0,1:T(8,128)(2,1)S(1)}, bf16[256,20]{0,1:T(8,128)(2,1)S(1)}, u32[]{:S(2)}, u32[]{:S(2)}) collective-permute-start(bf16[256,20]{0,1:T(8,128)(2,1)S(1)} %get-tuple-element.136), channel_id=1, source_target_pairs={{0,16},{16,32},{32,48},{48,64},{64,80},{80,96},{96,112},{1,17},{17... | collective-permute-start | bytes 30728 | tf_op jit(solution)/shard_map/ppermute | solution.py:21
  14.2 15.9 %copy-start.3 = (bf16[256,2560]{0,1:T(8,128)(2,1)}, bf16[256,2560]{0,1:T(8,128)(2,1)S(1)}, u32[]{:S(2)}) copy-start(bf16[256,2560]{0,1:T(8,128)(2,1)S(1)} %copy.15) | copy-start | bytes 3932164
  27.8 3.3 %slice-start = ((s8[5242880]{0:T(1024)(128)(4,1)}), s8[4194304]{0:T(1024)(128)(4,1)S(1)}, s32[]{:S(2)}) async-start(s8[5242880]{0:T(1024)(128)(4,1)} %bitcast.101), calls=%async_computation.1 | async-start | bytes 8388608
  29.6 1.5 copy-start.1
  29.6 2.2 slice-start.1
  31.8 2.4 copy-start.11
  31.8 3.3 %copy-start.10 = (f32[1,2560]{1,0:T(1,128)S(1)}, f32[1,2560]{1,0:T(1,128)}, u32[]{:S(2)}) copy-start(f32[1,2560]{1,0:T(1,128)} %param.14) | copy-start | bytes 30724
  109.2 5.9 %copy-start.5 = (f32[4,5,256]{2,1,0:T(8,128)S(1)}, f32[4,5,256]{2,1,0:T(8,128)}, u32[]{:S(2)}) copy-start(f32[4,5,256]{2,1,0:T(8,128)} %get-tuple-element.232) | copy-start | bytes 61444 | tf_op jit(solution)/shard_map/while
  115.0 6.7 %copy-start.6 = (f32[4,5,256]{2,1,0:T(8,128)S(1)}, f32[4,5,256]{2,1,0:T(8,128)}, u32[]{:S(2)}) copy-start(f32[4,5,256]{2,1,0:T(8,128)} %get-tuple-element.233) | copy-start | bytes 61444 | tf_op jit(solution)/shard_map/while
  115.0 7.0 %copy-start = (f32[4,512,256,5]{2,1,3,0:T(8,128)S(1)}, f32[4,512,256,5]{2,1,3,0:T(8,128)}, u32[]{:S(2)}) copy-start(f32[4,512,256,5]{2,1,3,0:T(8,128)} %get-tuple-element.216) | copy-start | bytes 31457284 | tf_op jit(solution)/shard_map/while
  121.7 5.2 %copy-start.7 = (f32[4,5,256]{2,1,0:T(8,128)}, f32[4,5,256]{2,1,0:T(8,128)S(1)}, u32[]{:S(2)}) copy-start(f32[4,5,256]{2,1,0:T(8,128)S(1)} %get-tuple-element.244) | copy-start | bytes 61444 | tf_op jit(solution)/shard_map/while
  131.2 5.9 %copy-start.5 = (f32[4,5,256]{2,1,0:T(8,128)S(1)}, f32[4,5,256]{2,1,0:T(8,128)}, u32[]{:S(2)}) copy-start(f32[4,5,256]{2,1,0:T(8,128)} %get-tuple-element.232) | copy-start | bytes 61444 | tf_op jit(solution)/shard_map/while
  137.0 6.7 %copy-start.6 = (f32[4,5,256]{2,1,0:T(8,128)S(1)}, f32[4,5,256]{2,1,0:T(8,128)}, u32[]{:S(2)}) copy-start(f32[4,5,256]{2,1,0:T(8,128)} %get-tuple-element.233) | copy-start | bytes 61444 | tf_op jit(solution)/shard_map/while
  137.0 7.0 %copy-start = (f32[4,512,256,5]{2,1,3,0:T(8,128)S(1)}, f32[4,512,256,5]{2,1,3,0:T(8,128)}, u32[]{:S(2)}) copy-start(f32[4,512,256,5]{2,1,3,0:T(8,128)} %get-tuple-element.216) | copy-start | bytes 31457284 | tf_op jit(solution)/shard_map/while
  143.7 6.6 %copy-start.7 = (f32[4,5,256]{2,1,0:T(8,128)}, f32[4,5,256]{2,1,0:T(8,128)S(1)}, u32[]{:S(2)}) copy-start(f32[4,5,256]{2,1,0:T(8,128)S(1)} %get-tuple-element.244) | copy-start | bytes 61444 | tf_op jit(solution)/shard_map/while
  154.6 5.9 %copy-start.5 = (f32[4,5,256]{2,1,0:T(8,128)S(1)}, f32[4,5,256]{2,1,0:T(8,128)}, u32[]{:S(2)}) copy-start(f32[4,5,256]{2,1,0:T(8,128)} %get-tuple-element.232) | copy-start | bytes 61444 | tf_op jit(solution)/shard_map/while
  160.4 6.7 %copy-start.6 = (f32[4,5,256]{2,1,0:T(8,128)S(1)}, f32[4,5,256]{2,1,0:T(8,128)}, u32[]{:S(2)}) copy-start(f32[4,5,256]{2,1,0:T(8,128)} %get-tuple-element.233) | copy-start | bytes 61444 | tf_op jit(solution)/shard_map/while
  160.5 7.0 %copy-start = (f32[4,512,256,5]{2,1,3,0:T(8,128)S(1)}, f32[4,512,256,5]{2,1,3,0:T(8,128)}, u32[]{:S(2)}) copy-start(f32[4,512,256,5]{2,1,3,0:T(8,128)} %get-tuple-element.216) | copy-start | bytes 31457284 | tf_op jit(solution)/shard_map/while
  167.2 6.6 %copy-start.7 = (f32[4,5,256]{2,1,0:T(8,128)}, f32[4,5,256]{2,1,0:T(8,128)S(1)}, u32[]{:S(2)}) copy-start(f32[4,5,256]{2,1,0:T(8,128)S(1)} %get-tuple-element.244) | copy-start | bytes 61444 | tf_op jit(solution)/shard_map/while
  178.0 5.9 %copy-start.5 = (f32[4,5,256]{2,1,0:T(8,128)S(1)}, f32[4,5,256]{2,1,0:T(8,128)}, u32[]{:S(2)}) copy-start(f32[4,5,256]{2,1,0:T(8,128)} %get-tuple-element.232) | copy-start | bytes 61444 | tf_op jit(solution)/shard_map/while
  183.9 6.7 %copy-start.6 = (f32[4,5,256]{2,1,0:T(8,128)S(1)}, f32[4,5,256]{2,1,0:T(8,128)}, u32[]{:S(2)}) copy-start(f32[4,5,256]{2,1,0:T(8,128)} %get-tuple-element.233) | copy-start | bytes 61444 | tf_op jit(solution)/shard_map/while
  183.9 7.0 %copy-start = (f32[4,512,256,5]{2,1,3,0:T(8,128)S(1)}, f32[4,512,256,5]{2,1,3,0:T(8,128)}, u32[]{:S(2)}) copy-start(f32[4,512,256,5]{2,1,3,0:T(8,128)} %get-tuple-element.216) | copy-start | bytes 31457284 | tf_op jit(solution)/shard_map/while
  190.6 6.6 %copy-start.7 = (f32[4,5,256]{2,1,0:T(8,128)}, f32[4,5,256]{2,1,0:T(8,128)S(1)}, u32[]{:S(2)}) copy-start(f32[4,5,256]{2,1,0:T(8,128)S(1)} %get-tuple-element.244) | copy-start | bytes 61444 | tf_op jit(solution)/shard_map/while
  201.4 5.9 %copy-start.5 = (f32[4,5,256]{2,1,0:T(8,128)S(1)}, f32[4,5,256]{2,1,0:T(8,128)}, u32[]{:S(2)}) copy-start(f32[4,5,256]{2,1,0:T(8,128)} %get-tuple-element.232) | copy-start | bytes 61444 | tf_op jit(solution)/shard_map/while
  207.3 6.7 %copy-start.6 = (f32[4,5,256]{2,1,0:T(8,128)S(1)}, f32[4,5,256]{2,1,0:T(8,128)}, u32[]{:S(2)}) copy-start(f32[4,5,256]{2,1,0:T(8,128)} %get-tuple-element.233) | copy-start | bytes 61444 | tf_op jit(solution)/shard_map/while
  207.3 7.0 %copy-start = (f32[4,512,256,5]{2,1,3,0:T(8,128)S(1)}, f32[4,512,256,5]{2,1,3,0:T(8,128)}, u32[]{:S(2)}) copy-start(f32[4,512,256,5]{2,1,3,0:T(8,128)} %get-tuple-element.216) | copy-start | bytes 31457284 | tf_op jit(solution)/shard_map/while
  214.0 6.6 %copy-start.7 = (f32[4,5,256]{2,1,0:T(8,128)}, f32[4,5,256]{2,1,0:T(8,128)S(1)}, u32[]{:S(2)}) copy-start(f32[4,5,256]{2,1,0:T(8,128)S(1)} %get-tuple-element.244) | copy-start | bytes 61444 | tf_op jit(solution)/shard_map/while
  224.9 5.9 %copy-start.5 = (f32[4,5,256]{2,1,0:T(8,128)S(1)}, f32[4,5,256]{2,1,0:T(8,128)}, u32[]{:S(2)}) copy-start(f32[4,5,256]{2,1,0:T(8,128)} %get-tuple-element.232) | copy-start | bytes 61444 | tf_op jit(solution)/shard_map/while
  230.7 6.7 %copy-start.6 = (f32[4,5,256]{2,1,0:T(8,128)S(1)}, f32[4,5,256]{2,1,0:T(8,128)}, u32[]{:S(2)}) copy-start(f32[4,5,256]{2,1,0:T(8,128)} %get-tuple-element.233) | copy-start | bytes 61444 | tf_op jit(solution)/shard_map/while
  230.7 7.0 %copy-start = (f32[4,512,256,5]{2,1,3,0:T(8,128)S(1)}, f32[4,512,256,5]{2,1,3,0:T(8,128)}, u32[]{:S(2)}) copy-start(f32[4,512,256,5]{2,1,3,0:T(8,128)} %get-tuple-element.216) | copy-start | bytes 31457284 | tf_op jit(solution)/shard_map/while
  237.4 6.6 %copy-start.7 = (f32[4,5,256]{2,1,0:T(8,128)}, f32[4,5,256]{2,1,0:T(8,128)S(1)}, u32[]{:S(2)}) copy-start(f32[4,5,256]{2,1,0:T(8,128)S(1)} %get-tuple-element.244) | copy-start | bytes 61444 | tf_op jit(solution)/shard_map/while
  248.3 5.9 %copy-start.5 = (f32[4,5,256]{2,1,0:T(8,128)S(1)}, f32[4,5,256]{2,1,0:T(8,128)}, u32[]{:S(2)}) copy-start(f32[4,5,256]{2,1,0:T(8,128)} %get-tuple-element.232) | copy-start | bytes 61444 | tf_op jit(solution)/shard_map/while
  254.2 6.7 %copy-start.6 = (f32[4,5,256]{2,1,0:T(8,128)S(1)}, f32[4,5,256]{2,1,0:T(8,128)}, u32[]{:S(2)}) copy-start(f32[4,5,256]{2,1,0:T(8,128)} %get-tuple-element.233) | copy-start | bytes 61444 | tf_op jit(solution)/shard_map/while
  254.2 7.0 %copy-start = (f32[4,512,256,5]{2,1,3,0:T(8,128)S(1)}, f32[4,512,256,5]{2,1,3,0:T(8,128)}, u32[]{:S(2)}) copy-start(f32[4,512,256,5]{2,1,3,0:T(8,128)} %get-tuple-element.216) | copy-start | bytes 31457284 | tf_op jit(solution)/shard_map/while
  260.9 6.6 %copy-start.7 = (f32[4,5,256]{2,1,0:T(8,128)}, f32[4,5,256]{2,1,0:T(8,128)S(1)}, u32[]{:S(2)}) copy-start(f32[4,5,256]{2,1,0:T(8,128)S(1)} %get-tuple-element.244) | copy-start | bytes 61444 | tf_op jit(solution)/shard_map/while
  271.7 5.9 %copy-start.5 = (f32[4,5,256]{2,1,0:T(8,128)S(1)}, f32[4,5,256]{2,1,0:T(8,128)}, u32[]{:S(2)}) copy-start(f32[4,5,256]{2,1,0:T(8,128)} %get-tuple-element.232) | copy-start | bytes 61444 | tf_op jit(solution)/shard_map/while
  277.6 6.7 %copy-start.6 = (f32[4,5,256]{2,1,0:T(8,128)S(1)}, f32[4,5,256]{2,1,0:T(8,128)}, u32[]{:S(2)}) copy-start(f32[4,5,256]{2,1,0:T(8,128)} %get-tuple-element.233) | copy-start | bytes 61444 | tf_op jit(solution)/shard_map/while
  277.6 7.0 %copy-start = (f32[4,512,256,5]{2,1,3,0:T(8,128)S(1)}, f32[4,512,256,5]{2,1,3,0:T(8,128)}, u32[]{:S(2)}) copy-start(f32[4,512,256,5]{2,1,3,0:T(8,128)} %get-tuple-element.216) | copy-start | bytes 31457284 | tf_op jit(solution)/shard_map/while
  284.3 6.6 %copy-start.7 = (f32[4,5,256]{2,1,0:T(8,128)}, f32[4,5,256]{2,1,0:T(8,128)S(1)}, u32[]{:S(2)}) copy-start(f32[4,5,256]{2,1,0:T(8,128)S(1)} %get-tuple-element.244) | copy-start | bytes 61444 | tf_op jit(solution)/shard_map/while
  291.5 2.2 copy-start.8
  293.7 1.7 copy-start.2
  293.7 2.1 copy-start.4
Sparse Core Ops, SparseCore 0:
  34.3 70.5 all-gather.1
where the time goes:
time: 310 us; the launch traced here: 305 us
  matrix products  106 us (34%)
  waiting for transfers between devices  73 us (24%)
  other arithmetic  66.2 us (21%)
  local copies, waits for them, and re-layouts  40.9 us (13%)
  between operations  13.6 us (4%)
  starting transfers between devices  3.84 us (1%)
    all_gather x1, waiting for transfers between devices, per_device(): key_value_rows = lax.all_gather(key_value_pair, 'ctx', axis=0, tiled=True)  59.5 us
    reduce_sum x8, other arithmetic, scores_step(): totals = totals * rescale + jnp.sum(weights, axis=-1)  53.2 us
    dot_general x8, matrix products, scores_step(): jnp.einsum('kgrs,skd->kgrd', weights.astype(jnp.bfloat16), value_portion,...  49.1 us
    dot_general x8, matrix products, scores_step(): jnp.einsum('rkgd,skd->kgrs', query_matrix, key_portion, preferred_element...  46.7 us
    dynamic_slice x24, local copies, waits for them, and re-layouts, per_device(): state_next, unused = lax.scan(visit, initial, blocks)  20.7 us
    ppermute x2, waiting for transfers between devices, shifted(): return lax.ppermute(x, axis, pairs)  13.5 us
    dot_general x1, matrix products, per_device(): jnp.dot(normed, q_weight[0], preferred_element_type=jnp.float32)  8.3 us
    while x72, local copies, waits for them, and re-layouts  7.02 us
  transfers between devices with their start and end apart: 3, of which 2 were waited for; matrix products, arithmetic and copies ran while one was open for 4% of the time, Pallas kernels for 0%

commit v1 on v0

v1 whole, which is shorter than its diff:
```python
import functools
import math

import jax
import jax.numpy as jnp
from jax import lax
from jax.experimental import pallas as pl
from jax.experimental.pallas import tpu as pltpu
from jax.sharding import PartitionSpec as P

MESH = pl.DeviceIdType.MESH
QUERY_HEADS = 20
KEY_VALUE_HEADS = 4
GROUP = QUERY_HEADS // KEY_VALUE_HEADS
HEAD_DIM = 128
QBLOCK = 128
EPSILON = 1e-06
MASK_FILLER = -1e30
SIDE = 4
ROWS = 256
MODEL = 2560
HEAD_COLS = GROUP * HEAD_DIM
LANES = GROUP * ROWS
CHUNK = 512
N_CHUNK = MODEL // CHUNK
KV_ROWS = 2 * ROWS
SUM_ROWS = 16
SCORE_LIMIT = 48.0
VALUE_LIMIT = 1e15

NT = (((1,), (1,)), ((), ()))
NN = (((1,), (0,)), ((), ()))


def dotf(left, right, dims=NN):
    return lax.dot_general(left, right, dims, preferred_element_type=jnp.float32)


def placement():
    section, ctx = lax.axis_index("section"), lax.axis_index("ctx")
    core = section % 2
    stride_a, stride_b = 1 + 3 * core, 4 - 3 * core
    x, y = ctx // SIDE, ctx % SIDE
    a = x * core + y * (1 - core)
    b = y * core + x * (1 - core)
    return section, ctx, a, b, stride_a, stride_b


def exchange_kernel(
    embedded, finished, gain, q_weight, kv_weight,
    q_all, kv_all, hidden_out,
    raw, hidden, scaled, q_w, kv_w, q_sum, kv_sum, square_sum, q_out, kv_out,
    raw_send, raw_recv, w_sem, local_sem,
    kv_send, kv_recv, row_send, row_recv, q_send, q_recv,
):
    section, ctx, a, b, stride_a, stride_b = placement()

    def at(a_to, b_to):
        return (section, a_to * stride_a + b_to * stride_b)

    def own_chunk(k):
        cols = pl.ds(pl.multiple_of(k * CHUNK, CHUNK), CHUNK)
        return pltpu.make_async_copy(embedded.at[:, cols], raw.at[:, cols], raw_recv.at[k])

    def hand_off(k):
        cols = pl.ds(pl.multiple_of(k * CHUNK, CHUNK), CHUNK)
        return pltpu.make_async_remote_copy(
            finished.at[:, cols], raw.at[:, cols], raw_send.at[k], raw_recv.at[k],
            device_id=((section + 1) % 8, ctx), device_id_type=MESH,
        )

    def weight_copies(k):
        rows = pl.ds(pl.multiple_of(k * CHUNK, CHUNK), CHUNK)
        return (
            pltpu.make_async_copy(kv_weight.at[rows, :], kv_w.at[rows, :], w_sem.at[0, k]),
            pltpu.make_async_copy(q_weight.at[rows, :], q_w.at[rows, :], w_sem.at[1, k]),
        )

    @pl.when(section == 0)
    def _():
        for k in range(N_CHUNK):
            own_chunk(k).start()

    barrier = pltpu.get_barrier_semaphore()
    for d in range(1, SIDE):
        for peer in (at((a + d) % SIDE, b), at(a, (b + d) % SIDE)):
            pl.semaphore_signal(barrier, inc=1, device_id=peer, device_id_type=MESH)

    @pl.when(section > 0)
    def _():
        pl.semaphore_signal(barrier, inc=1, device_id=(section - 1, ctx), device_id_type=MESH)

    @pl.when(section < 7)
    def _():
        pl.semaphore_signal(barrier, inc=1, device_id=(section + 1, ctx), device_id_type=MESH)

    for k in range(N_CHUNK):
        for copy in weight_copies(k):
            copy.start()

    @pl.when(jnp.logical_and(section > 0, section < 7))
    def _():
        pl.semaphore_wait(barrier, 8)

    @pl.when(jnp.logical_or(section == 0, section == 7))
    def _():
        pl.semaphore_wait(barrier, 7)

    @pl.when(section < 7)
    def _():
        for k in range(N_CHUNK):
            hand_off(k).start()

    kv_sum[...] = jnp.zeros_like(kv_sum)
    q_sum[...] = jnp.zeros_like(q_sum)
    square_sum[...] = jnp.zeros_like(square_sum)
    first = section == 0

    def take_chunk(k):
        @pl.when(section == 0)
        def _():
            own_chunk(k).wait()

        @pl.when(section > 0)
        def _():
            hand_off(k).wait_recv()

        squares = jnp.zeros((ROWS, QBLOCK), jnp.float32)
        for j in range(CHUNK // QBLOCK):
            cols = pl.ds(pl.multiple_of(k * CHUNK + j * QBLOCK, QBLOCK), QBLOCK)
            block = raw[:, cols].astype(jnp.float32)
            scale = (jnp.max(jnp.abs(block), axis=1, keepdims=True) + EPSILON).astype(jnp.bfloat16)
            scale = scale.astype(jnp.float32)
            coded = (block / scale).astype(jnp.bfloat16).astype(jnp.float32)
            rows = jnp.where(first, block, coded * scale)
            hidden[:, cols] = rows
            squares += rows * rows
            scaled[:, cols] = (rows * gain[0:1, cols]).astype(jnp.bfloat16)
        square_sum[...] += squares

    def add_kv(k):
        part = pl.ds(pl.multiple_of(k * CHUNK, CHUNK), CHUNK)
        weight_copies(k)[0].wait()
        kv_sum[...] += dotf(scaled[:, part], kv_w[part, :])

    def add_q(k):
        part = pl.ds(pl.multiple_of(k * CHUNK, CHUNK), CHUNK)
        weight_copies(k)[1].wait()
        for h in range(KEY_VALUE_HEADS):
            cols = slice(h * HEAD_COLS, (h + 1) * HEAD_COLS)
            q_sum[:, cols] += dotf(scaled[:, part], q_w[part, cols])

    def early(k, carry):
        take_chunk(k)
        add_kv(k)
        add_q(k)
        return carry

    lax.fori_loop(0, N_CHUNK - 1, early, 0)
    take_chunk(N_CHUNK - 1)
    hidden_copy = pltpu.make_async_copy(hidden, hidden_out, local_sem.at[0])
    hidden_copy.start()
    add_kv(N_CHUNK - 1)

    mean = jnp.sum(square_sum[...], axis=1, keepdims=True) * (1.0 / MODEL)
    inverse = lax.rsqrt(mean + EPSILON)
    for h in range(KEY_VALUE_HEADS):
        keys = kv_sum[:, h * HEAD_DIM:(h + 1) * HEAD_DIM] * inverse
        kv_out[h, 0:ROWS, :] = keys.astype(jnp.bfloat16)
        first_col = (KEY_VALUE_HEADS + h) * HEAD_DIM
        values = kv_sum[:, first_col:first_col + HEAD_DIM] * inverse
        turned = values.T.astype(jnp.bfloat16)
        kv_out[h, ROWS:ROWS + 128, :] = turned[:, 0:128]
        kv_out[h, ROWS + 128:ROWS + 256, :] = turned[:, 128:256]

    def kv_copy(d):
        return pltpu.make_async_remote_copy(
            kv_out.at[(a + d) % SIDE], kv_all.at[b, a], kv_send.at[d - 1], kv_recv.at[d - 1],
            device_id=at((a + d) % SIDE, b), device_id_type=MESH,
        )

    def row_copy(e, p, source):
        return pltpu.make_async_remote_copy(
            source, kv_all.at[b, (a + SIDE - p) % SIDE], row_send.at[e - 1, p], row_recv.at[e - 1, p],
            device_id=at(a, (b + e) % SIDE), device_id_type=MESH,
        )

    for d in (2, 1, 3):
        kv_copy(d).start()
    own_kv = pltpu.make_async_copy(kv_out.at[a], kv_all.at[b, a], local_sem.at[1])
    own_kv.start()
    for e in (2, 1, 3):
        row_copy(e, 0, kv_out.at[a]).start()

    add_q(N_CHUNK - 1)
    q_scale = inverse * (HEAD_DIM ** -0.5 * math.log2(math.e))
    for h in range(KEY_VALUE_HEADS):
        for g in range(GROUP):
            cols = slice((h * GROUP + g) * HEAD_DIM, (h * GROUP + g + 1) * HEAD_DIM)
            q_out[h, g * ROWS:(g + 1) * ROWS, :] = (q_sum[:, cols] * q_scale).astype(jnp.bfloat16)

    def q_copy(d):
        return pltpu.make_async_remote_copy(
            q_out.at[(a + d) % SIDE], q_all.at[SIDE - d], q_send.at[d - 1], q_recv.at[d - 1],
            device_id=at((a + d) % SIDE, b), device_id_type=MESH,
        )

    for d in (2, 1, 3):
        q_copy(d).start()
    own_q = pltpu.make_async_copy(q_out.at[a], q_all.at[0], local_sem.at[2])
    own_q.start()

    for p in (1, 3, 2):
        kv_copy(p).wait_recv()
        for e in (2, 1, 3):
            row_copy(e, p, kv_all.at[b, (a + SIDE - p) % SIDE]).start()

    hidden_copy.wait()
    own_kv.wait()
    own_q.wait()
    for d in range(1, SIDE):
        q_copy(d).wait()
        kv_copy(d).wait_send()
        for p in range(SIDE):
            row_copy(d, p, kv_out.at[a]).wait()

    @pl.when(section < 7)
    def _():
        for k in range(N_CHUNK):
            hand_off(k).wait_send()


def exchange(embedded, finished, gain, q_weight, kv_weight):
    any_spec = pl.BlockSpec(memory_space=pl.ANY)
    vmem = pltpu.VMEM
    dma = pltpu.SemaphoreType.DMA
    return pl.pallas_call(
        exchange_kernel,
        out_shape=(
            jax.ShapeDtypeStruct((SIDE, LANES, HEAD_DIM), jnp.bfloat16),
            jax.ShapeDtypeStruct((SIDE, SIDE, KV_ROWS, HEAD_DIM), jnp.bfloat16),
            jax.ShapeDtypeStruct((ROWS, MODEL), jnp.float32),
        ),
        in_specs=[any_spec, any_spec, pl.BlockSpec(memory_space=vmem), any_spec, any_spec],
        out_specs=(any_spec, any_spec, any_spec),
        scratch_shapes=[
            vmem((ROWS, MODEL), jnp.bfloat16),
            vmem((ROWS, MODEL), jnp.float32),
            vmem((ROWS, MODEL), jnp.bfloat16),
            vmem((MODEL, MODEL), jnp.bfloat16),
            vmem((MODEL, 2 * KEY_VALUE_HEADS * HEAD_DIM), jnp.bfloat16),
            vmem((ROWS, MODEL), jnp.float32),
            vmem((ROWS, 2 * KEY_VALUE_HEADS * HEAD_DIM), jnp.float32),
            vmem((ROWS, QBLOCK), jnp.float32),
            vmem((SIDE, LANES, HEAD_DIM), jnp.bfloat16),
            vmem((SIDE, KV_ROWS, HEAD_DIM), jnp.bfloat16),
            dma((N_CHUNK,)), dma((N_CHUNK,)), dma((2, N_CHUNK)), dma((3,)),
            dma((3,)), dma((3,)), dma((3, SIDE)), dma((3, SIDE)), dma((3,)), dma((3,)),
        ],
        compiler_params=pltpu.CompilerParams(
            collective_id=0, has_side_effects=True, vmem_limit_bytes=48 << 20
        ),
        cost_estimate=pl.CostEstimate(
            flops=2 * ROWS * MODEL * 3584, bytes_accessed=24 << 20, transcendentals=0
        ),
    )(embedded, finished, gain, q_weight, kv_weight)


def attend_kernel(steps, order, q_hbm, kv_hbm, *refs):
    outs = refs[:len(steps)]
    queries, kv, total, peak, slot_of, flag, sems = refs[len(steps):]
    _, _, a, b, stride_a, stride_b = placement()
    kv_copy = pltpu.make_async_copy(kv_hbm, kv, sems.at[0])
    kv_copy.start()
    q_copies = [
        pltpu.make_async_copy(q_hbm.at[e], queries.at[i], sems.at[1 + i]) for i, e in enumerate(steps)
    ]
    for copy in q_copies:
        copy.start()
    for b_of in range(SIDE):
        for a_of in range(SIDE):
            slot_of[order[a_of * stride_a + b_of * stride_b]] = b_of * SIDE + a_of

    kv_copy.wait()
    for copy in q_copies:
        copy.wait()

    ones = jnp.ones((SUM_ROWS, HEAD_DIM), jnp.bfloat16)

    def longest(rows):
        wide = rows.astype(jnp.float32)
        return jnp.max(dotf(ones, (wide * wide).astype(jnp.bfloat16), NT))

    def widest(slot, most):
        values = kv[slot, ROWS:KV_ROWS, :]
        return (
            jnp.maximum(most[0], longest(kv[slot, 0:ROWS, :])),
            jnp.maximum(most[1], jnp.max(jnp.abs(values.astype(jnp.float32)))),
        )

    k_most, v_most = lax.fori_loop(0, SIDE * SIDE, widest, (jnp.float32(0), jnp.float32(0)))
    q_most = lax.fori_loop(
        0, len(steps), lambda i, most: jnp.maximum(most, longest(queries[i])), jnp.float32(0)
    )
    small = jnp.logical_and(
        q_most * k_most <= SCORE_LIMIT * SCORE_LIMIT, v_most <= VALUE_LIMIT
    )

    def key_rows(slots):
        return jnp.concatenate([kv[slot, 0:ROWS, :] for slot in slots], axis=0)

    def value_cols(slots):
        parts = []
        for slot in slots:
            for half in range(2):
                first = ROWS + half * HEAD_DIM
                parts.append(jnp.concatenate([kv[slot, first:first + HEAD_DIM, :], ones], axis=0))
        return jnp.concatenate(parts, axis=1)

    def causal():
        key = lax.broadcasted_iota(jnp.int32, (ROWS, LANES), 0)
        query = lax.broadcasted_iota(jnp.int32, (ROWS, LANES), 1) % ROWS
        return key <= query

    for i, e in enumerate(steps):
        rank = order[((a + e) % SIDE) * stride_a + b * stride_b]

        @pl.when(small)
        def _():
            total[...] = jnp.zeros_like(total)

            def four(c, carry):
                slots = [slot_of[4 * c + j] for j in range(4)]
                weights = jnp.exp2(dotf(key_rows(slots), queries[i], NT)).astype(jnp.bfloat16)
                total[...] += dotf(value_cols(slots), weights)
                return carry

            lax.fori_loop(0, rank // 4, four, 0)
            for rest in range(4):

                @pl.when(rank % 4 == rest)
                def _():
                    slots = [slot_of[rank - rest + j] for j in range(rest + 1)]
                    weights = jnp.exp2(dotf(key_rows(slots), queries[i], NT))
                    last = jnp.where(causal(), weights[rest * ROWS:, :], 0.0)
                    if rest:
                        last = jnp.concatenate([weights[:rest * ROWS, :], last], axis=0)
                    total[...] += dotf(value_cols(slots), last.astype(jnp.bfloat16))

        @pl.when(jnp.logical_not(small))
        def _():
            total[...] = jnp.zeros_like(total)
            peak[...] = jnp.full_like(peak, MASK_FILLER)

            def one(t, carry):
                slots = [slot_of[t]]
                scores = dotf(key_rows(slots), queries[i], NT)
                visible = jnp.logical_or(causal(), t < rank)
                scores = jnp.where(visible, scores, MASK_FILLER)
                before = peak[0:1, :]
                now = jnp.maximum(before, jnp.max(scores, axis=0, keepdims=True))
                weights = jnp.where(visible, jnp.exp2(scores - now), 0.0)
                total[...] = total[...] * jnp.exp2(before - now) + dotf(
                    value_cols(slots), weights.astype(jnp.bfloat16)
                )
                peak[0:1, :] = now
                return carry

            lax.fori_loop(0, rank + 1, one, 0)

        for g in range(GROUP):
            lanes = slice(g * ROWS, (g + 1) * ROWS)
            share = total[0:HEAD_DIM, lanes] / total[HEAD_DIM:HEAD_DIM + 1, lanes]
            outs[i][:, g * HEAD_DIM:(g + 1) * HEAD_DIM] = share.T.astype(jnp.bfloat16)


def attend(order, q_all, kv_all, steps):
    any_spec = pl.BlockSpec(memory_space=pl.ANY)
    vmem = pltpu.VMEM
    out = jax.ShapeDtypeStruct((ROWS, HEAD_COLS), jnp.bfloat16)
    n = len(steps)
    return pl.pallas_call(
        functools.partial(attend_kernel, steps),
        out_shape=(out,) * n,
        in_specs=[pl.BlockSpec(memory_space=pltpu.SMEM), any_spec, any_spec],
        out_specs=(pl.BlockSpec(memory_space=vmem),) * n,
        scratch_shapes=[
            vmem((n, LANES, HEAD_DIM), jnp.bfloat16),
            vmem((SIDE * SIDE, KV_ROWS, HEAD_DIM), jnp.bfloat16),
            vmem((HEAD_DIM + SUM_ROWS, LANES), jnp.float32),
            vmem((8, LANES), jnp.float32),
            pltpu.SMEM((SIDE * SIDE,), jnp.int32),
            pltpu.SMEM((1,), jnp.int32),
            pltpu.SemaphoreType.DMA((1 + n,)),
        ],
        compiler_params=pltpu.CompilerParams(vmem_limit_bytes=48 << 20),
        cost_estimate=pl.CostEstimate(
            flops=n * 4 * LANES * HEAD_DIM * 2304, bytes_accessed=3 << 20, transcendentals=n * LANES * 2304
        ),
    )(order, q_all, kv_all.reshape(SIDE * SIDE, KV_ROWS, HEAD_DIM))


def finish_kernel(p0, p1, p2, p3, hidden, gain, out):
    _, _, a, _, _, _ = placement()
    pieces = [p[...].astype(jnp.float32) for p in (p0, p1, p2, p3)]
    squares = sum(jnp.sum(p * p, axis=1, keepdims=True) for p in pieces)
    inverse = lax.rsqrt(squares * (1.0 / MODEL) + EPSILON)
    for d, piece in enumerate(pieces):
        first = pl.multiple_of(((a + SIDE - d) % SIDE) * HEAD_COLS, HEAD_COLS)
        cols = pl.ds(first, HEAD_COLS)
        rows = hidden[:, cols] + gain[0:1, cols] * (piece * inverse)
        out[:, cols] = rows.astype(jnp.bfloat16)


def finish(pieces, hidden, gain):
    tile = 64
    piece = pl.BlockSpec((tile, HEAD_COLS), lambda i: (i, 0))
    whole = pl.BlockSpec((tile, MODEL), lambda i: (i, 0))
    return pl.pallas_call(
        finish_kernel,
        grid=(ROWS // tile,),
        out_shape=jax.ShapeDtypeStruct((ROWS, MODEL), jnp.bfloat16),
        in_specs=[piece] * 4 + [whole, pl.BlockSpec((1, MODEL), lambda i: (0, 0))],
        out_specs=whole,
    )(*pieces, hidden, gain)


def send_along(x, d):
    pairs = []
    for section in range(8):
        for ctx in range(16):
            if section % 2:
                to = (ctx + d * SIDE) % 16
            else:
                to = ctx // SIDE * SIDE + (ctx + d) % SIDE
            pairs.append((section * 16 + ctx, section * 16 + to))
    return lax.ppermute(x, ("section", "ctx"), pairs)


def per_device(embedded, finished, norm_gain, q_weight, kv_weight, out_gain, span_order):
    q_all, kv_all, hidden = exchange(
        embedded, finished[0], norm_gain, q_weight[0], kv_weight[0]
    )
    far, near, back = attend(span_order, q_all, kv_all, (2, 1, 3))
    far, near, back = send_along(far, 2), send_along(near, 1), send_along(back, 3)
    (own,) = attend(span_order, q_all, kv_all, (0,))
    return finish((own, near, far, back), hidden, out_gain)[None]


def solution(mesh):
    placed = (
        P("ctx", None),
        P("section", "ctx", None),
        P("section", None),
        P("section", None, None),
        P("section", None, None),
        P("section", None),
        P(),
    )
    return jax.shard_map(
        per_device, mesh=mesh, in_specs=placed, out_specs=P("section", "ctx", None), check_vma=False
    )
```

time: 310 us -> 111 us (0.36); the launches traced: 305 us -> 111 us
  matrix products: 106 us -> 0 us
  Pallas kernels: 0 us -> 92.6 us
  waiting for transfers between devices: 73 us -> 0.01 us
  other arithmetic: 66.2 us -> 0 us
  local copies, waits for them, and re-layouts: 40.9 us -> 5 us
  between operations: 13.6 us -> 0.08 us
  starting transfers between devices: 3.84 us -> 13.5 us
    dot_general x18 -> x0, matrix products: 106 us -> none  [the longest x8 49.1 us: scores_step(): jnp.einsum('kgrs,skd->kgrd', weights.astype(jnp.bfloat16), value_portion,...]
    pallas_call x0 -> x4, Pallas kernels: none -> 92.6 us  [the longest x2 49.5 us: attend(): pl.pallas_call(functools.partial(attend_kernel, steps), out_shape=(out,)...]
    all_gather x1 -> x0, waiting for transfers between devices: 59.5 us -> none  [per_device(): key_value_rows = lax.all_gather(key_value_pair, 'ctx', axis=0, tiled=True)]
    reduce_sum x10 -> x0, other arithmetic: 54.1 us -> none  [the longest x8 53.2 us: scores_step(): totals = totals * rescale + jnp.sum(weights, axis=-1)]
    dynamic_slice x25 -> x0, local copies, waits for them, and re-layouts: 21.3 us -> none  [the longest x24 20.7 us: per_device(): state_next, unused = lax.scan(visit, initial, blocks)]
    ppermute x2 -> x3, waiting for transfers between devices: 13.5 us -> 0.01 us  [send_along(): return lax.ppermute(x, ('section', 'ctx'), pairs)]
    ppermute x2 -> x3, starting transfers between devices: 3.84 us -> 13.5 us  [send_along(): return lax.ppermute(x, ('section', 'ctx'), pairs)]
    while x73 -> x0, local copies, waits for them, and re-layouts: 9.18 us -> none
  transfers between devices with their start and end apart: 3 -> 3, of which waited for: 2 -> 0; matrix products, arithmetic and copies ran while one was open for 4% -> 0% of each run, Pallas kernels for 0% -> 16%
where the time goes in v1:
time: 111 us
  Pallas kernels  92.6 us (83%)
  starting transfers between devices  13.5 us (12%)
  local copies, waits for them, and re-layouts  5 us (5%)
    pallas_call x2, Pallas kernels, attend(): pl.pallas_call(functools.partial(attend_kernel, steps), out_shape=(out,)...  49.5 us
    pallas_call x1, Pallas kernels, exchange(): pl.pallas_call(exchange_kernel, out_shape=(jax.ShapeDtypeStruct((SIDE, LA...  38.6 us
    ppermute x3, starting transfers between devices, send_along(): return lax.ppermute(x, ('section', 'ctx'), pairs)  13.5 us
    unnamed x16, local copies, waits for them, and re-layouts  5 us
    pallas_call x1, Pallas kernels, finish(): pl.pallas_call(finish_kernel, grid=(ROWS // tile,), out_shape=jax.ShapeDt...  4.47 us
  transfers between devices with their start and end apart: 3, of which 0 were waited for; matrix products, arithmetic and copies ran while one was open for 0% of the time, Pallas kernels for 16%

profile of v1, /device:TPU:106, one launch (start us, length us, event | category | flops | bytes accessed | tf_op | source)
XLA Modules:
  0.0 111.1 jit_solution(17625646367029323936)
XLA Ops:
  0.0 0.0 copy-start
  0.0 1.3 %copy-done = bf16[256,2560]{1,0:T(8,128)(2,1)S(1)} copy-done((bf16[256,2560]{1,0:T(8,128)(2,1)S(1)}, bf16[256,2560]{1,0:T(8,128)(2,1)}, u32[]{:S(2)}) %copy-start) | copy-done | bytes 1310744
  1.3 0.0 copy-start.1
  1.3 1.3 %copy-done.1 = bf16[1,256,2560]{2,1,0:T(8,128)(2,1)S(1)} copy-done((bf16[1,256,2560]{2,1,0:T(8,128)(2,1)S(1)}, bf16[1,256,2560]{2,1,0:T(8,128)(2,1)}, u32[]{:S(2)}) %copy-start.1) | copy-done | bytes 1310744
  2.6 0.0 copy-start.3
  2.6 0.7 copy-done.3
  3.3 0.0 copy-start.4
  3.3 38.6 %shard_map.73 = (bf16[4,1280,128]{2,1,0:T(8,128)(2,1)S(1)}, bf16[4,4,512,128]{3,2,1,0:T(8,128)(2,1)S(1)}, f32[256,2560]{1,0:T(8,128)}) custom-call(bf16[256,2560]{1,0:T(8,128)(2,1)S(1)} %copy-done, bf16[256,2560]{1,0:T(8,128)(2,1)S(1)} %bitcast.5, f32[1,2560]{1,0:T(1,128)S(1)} %copy-done.3, bf16[2560,2560]{1,0:T(8,128)(2,1)} %bitcast.8, ...), custom_call_target="tpu_custom_call" | custom-call | flops 4697620480 | bytes 25165824 | tf_op jit(solution)/shard_map/pallas_call | solution.py:237
  42.0 0.0 copy-done.4
  42.0 31.4 %shard_map.75 = (bf16[256,640]{1,0:T(8,128)(2,1)S(1)}, bf16[256,640]{1,0:T(8,128)(2,1)S(1)}, bf16[256,640]{1,0:T(8,128)(2,1)S(1)}) custom-call(s32[16]{0:T(128)S(1)} %copy-done.4, bf16[4,1280,128]{2,1,0:T(8,128)(2,1)S(1)} %get-tuple-element.11.q_hbm, bf16[16,512,128]{2,1,0:T(8,128)(2,1)S(1)} %bitcast.6), custom_call_target="tpu_custom_call" | custom-call | flops 4529848320 | bytes 3145728 | tf_op jit(solution)/shard_map/pallas_call | solution.py:382
  73.3 6.8 %collective-permute-start = (bf16[256,640]{1,0:T(8,128)(2,1)S(1)}, bf16[256,640]{1,0:T(8,128)(2,1)S(1)}, u32[]{:S(2)}, u32[]{:S(2)}) collective-permute-start(bf16[256,640]{1,0:T(8,128)(2,1)S(1)} %get-tuple-element.13), channel_id=1, source_target_pairs={{0,1},{1,2},{2,3},{3,0},{4,5},{5,6},{6,7},{7,4},{8,9},{9,10},{10,1... | collective-permute-start | bytes 983048 | tf_op jit(solution)/shard_map/ppermute | solution.py:437
  80.2 6.6 %collective-permute-start.1 = (bf16[256,640]{1,0:T(8,128)(2,1)S(1)}, bf16[256,640]{1,0:T(8,128)(2,1)S(1)}, u32[]{:S(2)}, u32[]{:S(2)}) collective-permute-start(bf16[256,640]{1,0:T(8,128)(2,1)S(1)} %get-tuple-element.14), channel_id=1, source_target_pairs={{0,2},{1,3},{2,0},{3,1},{4,6},{5,7},{6,4},{7,5},{8,10},{9,11},{10,... | collective-permute-start | bytes 983048 | tf_op jit(solution)/shard_map/ppermute | solution.py:437
  86.8 0.0 collective-permute-start.2
  86.8 18.2 %shard_map.74.p0 = bf16[256,640]{1,0:T(8,128)(2,1)S(1)} custom-call(s32[16]{0:T(128)S(1)} %copy-done.4, bf16[4,1280,128]{2,1,0:T(8,128)(2,1)S(1)} %get-tuple-element.11.q_hbm, bf16[16,512,128]{2,1,0:T(8,128)(2,1)S(1)} %bitcast.7), custom_call_target="tpu_custom_call" | custom-call | flops 1509949440 | bytes 3145728 | tf_op jit(solution)/shard_map/pallas_call | solution.py:382
  105.0 0.0 copy-start.2
  105.0 0.7 copy-done.2
  105.7 0.0 collective-permute-done.p1
  105.7 0.0 copy-start.5
  105.7 0.0 collective-permute-done.1.p2
  105.7 0.0 copy-start.6
  105.7 0.0 collective-permute-done.2.p3
  105.7 0.0 copy-start.7
  105.7 0.7 copy-done.5
  106.4 0.1 copy-done.6
  106.5 0.1 copy-done.7
  106.7 4.5 %shard_map.76 = bf16[256,2560]{1,0:T(8,128)(2,1)} custom-call(bf16[256,640]{1,0:T(8,128)(2,1)} %copy-done.2, bf16[256,640]{1,0:T(8,128)(2,1)} %copy-done.5, bf16[256,640]{1,0:T(8,128)(2,1)} %copy-done.6, bf16[256,640]{1,0:T(8,128)(2,1)} %copy-done.7, f32[256,2560]{1,0:T(8,128)} %get-tuple-element.16.hidden, f32[1,2560]{1,0:T(1,128)} %gain.3), custom_call_target="tpu_custom_call" | custom-call | tf_op jit(solution)/shard_map/pallas_call | solution.py:419
Async XLA Ops:
  0.0 1.3 %copy-start = (bf16[256,2560]{1,0:T(8,128)(2,1)S(1)}, bf16[256,2560]{1,0:T(8,128)(2,1)}, u32[]{:S(2)}) copy-start(bf16[256,2560]{1,0:T(8,128)(2,1)} %embedded.1) | copy-start | bytes 3932164
  1.3 1.3 %copy-start.1 = (bf16[1,256,2560]{2,1,0:T(8,128)(2,1)S(1)}, bf16[1,256,2560]{2,1,0:T(8,128)(2,1)}, u32[]{:S(2)}) copy-start(bf16[1,256,2560]{2,1,0:T(8,128)(2,1)} %param.8) | copy-start | bytes 3932164
  2.6 0.7 copy-start.3
  3.3 38.6 %copy-start.4 = (s32[16]{0:T(128)S(1)}, s32[16]{0:T(128)}, u32[]{:S(2)}) copy-start(s32[16]{0:T(128)} %order.3) | copy-start | bytes 196
  73.3 32.4 %collective-permute-start = (bf16[256,640]{1,0:T(8,128)(2,1)S(1)}, bf16[256,640]{1,0:T(8,128)(2,1)S(1)}, u32[]{:S(2)}, u32[]{:S(2)}) collective-permute-start(bf16[256,640]{1,0:T(8,128)(2,1)S(1)} %get-tuple-element.13), channel_id=1, source_target_pairs={{0,1},{1,2},{2,3},{3,0},{4,5},{5,6},{6,7},{7,4},{8,9},{9,10},{10,1... | collective-permute-start | bytes 983048 | tf_op jit(solution)/shard_map/ppermute | solution.py:437
  80.2 25.6 %collective-permute-start.1 = (bf16[256,640]{1,0:T(8,128)(2,1)S(1)}, bf16[256,640]{1,0:T(8,128)(2,1)S(1)}, u32[]{:S(2)}, u32[]{:S(2)}) collective-permute-start(bf16[256,640]{1,0:T(8,128)(2,1)S(1)} %get-tuple-element.14), channel_id=1, source_target_pairs={{0,2},{1,3},{2,0},{3,1},{4,6},{5,7},{6,4},{7,5},{8,10},{9,11},{10,... | collective-permute-start | bytes 983048 | tf_op jit(solution)/shard_map/ppermute | solution.py:437
  86.8 18.9 %collective-permute-start.2 = (bf16[256,640]{1,0:T(8,128)(2,1)S(1)}, bf16[256,640]{1,0:T(8,128)(2,1)S(1)}, u32[]{:S(2)}, u32[]{:S(2)}) collective-permute-start(bf16[256,640]{1,0:T(8,128)(2,1)S(1)} %get-tuple-element.15), channel_id=1, source_target_pairs={{0,3},{1,0},{2,1},{3,2},{4,7},{5,4},{6,5},{7,6},{8,11},{9,8},{10,9... | collective-permute-start | bytes 983048 | tf_op jit(solution)/shard_map/ppermute | solution.py:437
  105.0 0.7 copy-start.2
  105.7 0.7 copy-start.5
  105.7 0.8 copy-start.6
  105.7 0.9 copy-start.7

commit v2 on v1

v2 whole, which is shorter than its diff:
```python
import functools
import math

import jax
import jax.numpy as jnp
from jax import lax
from jax.experimental import pallas as pl
from jax.experimental.pallas import tpu as pltpu
from jax.sharding import PartitionSpec as P

MESH = pl.DeviceIdType.MESH
QUERY_HEADS = 20
KEY_VALUE_HEADS = 4
GROUP = QUERY_HEADS // KEY_VALUE_HEADS
HEAD_DIM = 128
QBLOCK = 128
EPSILON = 1e-06
MASK_FILLER = -1e30
SIDE = 4
ROWS = 256
HALF = ROWS // 2
MODEL = 2560
HEAD_COLS = GROUP * HEAD_DIM
LANES = GROUP * ROWS
CHUNK = 512
N_CHUNK = MODEL // CHUNK
SUM_ROWS = 16
KV_PART = 2 * HALF + SUM_ROWS
Q_PART = GROUP * HALF + SUM_ROWS
ORDER = (2, 1, 3, 0)
RELAYED, DIRECT = (0, 1), (2, 0, 1)
MARGIN = 1.02
Q_SCALE = HEAD_DIM ** -0.5 * math.log2(math.e)
SCORE_LIMIT = 48.0
VALUE_LIMIT = 1e15

NT = (((1,), (1,)), ((), ()))
NN = (((1,), (0,)), ((), ()))


def dotf(left, right, dims=NN):
    return lax.dot_general(left, right, dims, preferred_element_type=jnp.float32)


def placement():
    section, ctx = lax.axis_index("section"), lax.axis_index("ctx")
    core = section % 2
    stride_a, stride_b = 1 + 3 * core, 4 - 3 * core
    x, y = ctx // SIDE, ctx % SIDE
    a = x * core + y * (1 - core)
    b = y * core + x * (1 - core)
    return section, ctx, a, b, stride_a, stride_b


def exchange_kernel(
    embedded, finished, gain, q_weight, kv_weight,
    q_all, kv_all, hidden_out,
    raw, hidden, scaled, q_w, kv_w, q_sum, kv_sum, square_sum, q_out, kv_out,
    raw_send, raw_recv, w_sem, hidden_sem, own_sem,
    kv_send, kv_recv, row_send, row_recv, on_send, on_recv, q_send, q_recv,
):
    section, ctx, a, b, stride_a, stride_b = placement()
    everything = pl.ds(0, 2)

    def at(a_to, b_to):
        return (section, a_to * stride_a + b_to * stride_b)

    def area(i, k):
        return (
            pl.ds(i * HALF, HALF),
            pl.ds(pl.multiple_of(k * CHUNK, CHUNK), CHUNK),
        )

    def own_chunk(i, k):
        return pltpu.make_async_copy(embedded.at[area(i, k)], raw.at[area(i, k)], raw_recv.at[i, k])

    def hand_off(i, k):
        return pltpu.make_async_remote_copy(
            finished.at[area(i, k)], raw.at[area(i, k)], raw_send.at[i, k], raw_recv.at[i, k],
            device_id=((section + 1) % 8, ctx), device_id_type=MESH,
        )

    kv_weight_copy = pltpu.make_async_copy(kv_weight, kv_w, w_sem.at[SIDE])

    def q_weight_copy(d):
        h = (a + d) % SIDE
        cols = pl.ds(pl.multiple_of(h * HEAD_COLS, HEAD_COLS), HEAD_COLS)
        return pltpu.make_async_copy(q_weight.at[:, cols], q_w.at[h], w_sem.at[d])

    @pl.when(section == 0)
    def _():
        for i in range(2):
            for k in range(N_CHUNK):
                own_chunk(i, k).start()

    barrier = pltpu.get_barrier_semaphore()

    @pl.when(section > 0)
    def _():
        pl.semaphore_signal(barrier, inc=1, device_id=(section - 1, ctx), device_id_type=MESH)

    @pl.when(section < 7)
    def _():
        pl.semaphore_signal(barrier, inc=1, device_id=(section + 1, ctx), device_id_type=MESH)

    for d in range(1, SIDE):
        for peer in (at((a + d) % SIDE, b), at(a, (b + d) % SIDE)):
            pl.semaphore_signal(barrier, inc=1, device_id=peer, device_id_type=MESH)

    kv_weight_copy.start()
    for d in ORDER:
        q_weight_copy(d).start()

    @pl.when(jnp.logical_and(section > 0, section < 7))
    def _():
        pl.semaphore_wait(barrier, 8)

    @pl.when(jnp.logical_or(section == 0, section == 7))
    def _():
        pl.semaphore_wait(barrier, 7)

    @pl.when(section < 7)
    def _():
        for i in range(2):
            for k in range(N_CHUNK):
                hand_off(i, k).start()

    first = section == 0

    def take_chunk(i, k):
        @pl.when(section == 0)
        def _():
            own_chunk(i, k).wait()

        @pl.when(section > 0)
        def _():
            hand_off(i, k).wait_recv()

        rows = pl.ds(i * HALF, HALF)
        squares = jnp.zeros((HALF, QBLOCK), jnp.float32)
        for j in range(CHUNK // QBLOCK):
            cols = pl.ds(pl.multiple_of(k * CHUNK + j * QBLOCK, QBLOCK), QBLOCK)
            block = raw[rows, cols].astype(jnp.float32)
            scale = (jnp.max(jnp.abs(block), axis=1, keepdims=True) + EPSILON).astype(jnp.bfloat16)
            scale = scale.astype(jnp.float32)
            coded = (block / scale).astype(jnp.bfloat16).astype(jnp.float32)
            taken = jnp.where(first, block, coded * scale)
            hidden[rows, cols] = taken
            squares += taken * taken
            scaled[rows, cols] = (taken * gain[0:1, cols]).astype(jnp.bfloat16)
        square_sum[rows, :] += squares

    def inverse_rms(rows):
        mean = jnp.sum(square_sum[rows, :], axis=1, keepdims=True) * (1.0 / MODEL)
        return lax.rsqrt(mean + EPSILON)

    def filled(value):
        return jnp.broadcast_to(value * MARGIN, (SUM_ROWS // 2, HEAD_DIM))

    def longest_square(rows):
        return jnp.max(jnp.sum(rows * rows, axis=1, keepdims=True), axis=0, keepdims=True)

    def store_kv(i, sums, inverse):
        for h in range(KEY_VALUE_HEADS):
            keys = sums[:, h * HEAD_DIM:(h + 1) * HEAD_DIM] * inverse
            kv_out[h, i, 0:HALF, :] = keys.astype(jnp.bfloat16)
            first_col = (KEY_VALUE_HEADS + h) * HEAD_DIM
            values = sums[:, first_col:first_col + HEAD_DIM] * inverse
            kv_out[h, i, HALF:2 * HALF, :] = values.T.astype(jnp.bfloat16)
            largest = jnp.max(jnp.max(jnp.abs(values), axis=0, keepdims=True), axis=1, keepdims=True)
            bounds = jnp.concatenate([filled(longest_square(keys)), filled(largest)], axis=0)
            kv_out[h, i, 2 * HALF:, :] = bounds.astype(jnp.bfloat16)

    def store_q(h, i, sums, q_scale):
        most = jnp.zeros((1, 1), jnp.float32)
        for g in range(GROUP):
            queries = sums[:, g * HEAD_DIM:(g + 1) * HEAD_DIM] * q_scale
            q_out[h, i, g * HALF:(g + 1) * HALF, :] = queries.astype(jnp.bfloat16)
            most = jnp.maximum(most, longest_square(queries))
        q_out[h, i, GROUP * HALF:, :] = jnp.concatenate([filled(most)] * 2, axis=0).astype(jnp.bfloat16)

    def kv_copy(part, i, d):
        return pltpu.make_async_remote_copy(
            kv_out.at[(a + d) % SIDE, part], kv_all.at[b, a, part], kv_send.at[i, d - 1], kv_recv.at[i, d - 1],
            device_id=at((a + d) % SIDE, b), device_id_type=MESH,
        )

    def source(p):
        return (a + SIDE - p) % SIDE

    def row_copy(part, i, p, way):
        block = kv_out.at[a, part] if p == 0 else kv_all.at[b, source(p), part]
        return pltpu.make_async_remote_copy(
            block, kv_all.at[b, source(p), part], row_send.at[i, p, way], row_recv.at[i, p, way],
            device_id=at(a, (b + (1, 3, 2)[way]) % SIDE), device_id_type=MESH,
        )

    def on_copy(part, i, p):
        way = p % 2
        block = kv_all.at[(b + (3, 1)[way]) % SIDE, source(p), part]
        return pltpu.make_async_remote_copy(
            block, block, on_send.at[i, p], on_recv.at[i, p],
            device_id=at(a, (b + (1, 3)[way]) % SIDE), device_id_type=MESH,
        )

    def q_copy(part, i, d):
        return pltpu.make_async_remote_copy(
            q_out.at[(a + d) % SIDE, part], q_all.at[SIDE - d, part], q_send.at[i, d - 1], q_recv.at[i, d - 1],
            device_id=at((a + d) % SIDE, b), device_id_type=MESH,
        )

    def own_kv(part, i):
        return pltpu.make_async_copy(kv_out.at[a, part], kv_all.at[b, a, part], own_sem.at[0, i])

    def own_q(part, i):
        return pltpu.make_async_copy(q_out.at[a, part], q_all.at[0, part], own_sem.at[1, i])

    def hidden_copy(i):
        rows = pl.ds(i * HALF, HALF)
        return pltpu.make_async_copy(hidden.at[rows, :], hidden_out.at[rows, :], hidden_sem.at[i])

    def send_kv(part, i, ways):
        for d in (2, 1, 3):
            kv_copy(part, i, d).start()
        for way in ways:
            row_copy(part, i, 0, way).start()
        own_kv(part, i).start()

    def spread(part, i, ways):
        for p in (1, 3, 2):
            kv_copy(part, i, p).wait_recv()
            for way in ways:
                row_copy(part, i, p, way).start()

    def pass_on(part, i):
        for p in (0, 1, 3, 2):
            row_copy(part, i, p, p % 2).wait_recv()
            on_copy(part, i, p).start()

    def settle(part, i, ways):
        own_kv(part, i).wait()
        own_q(part, i).wait()
        for d in range(1, SIDE):
            q_copy(part, i, d).wait()
            kv_copy(part, i, d).wait_send()
        for p in range(SIDE):
            if len(ways) == 3:
                for way in ways:
                    row_copy(part, i, p, way).wait()
            else:
                row_copy(part, i, p, 1 - p % 2).wait_recv()
                for way in ways:
                    row_copy(part, i, p, way).wait_send()
                on_copy(part, i, p).wait()

    square_sum[...] = jnp.zeros_like(square_sum)
    waits = jnp.logical_and(section % 2 == 0, section > 0)

    @pl.when(waits)
    def _():
        def add_kv(i, k):
            part = pl.ds(pl.multiple_of(k * CHUNK, CHUNK), CHUNK)
            kv_sum[...] += dotf(scaled[pl.ds(i * HALF, HALF), part], kv_w[part, :])

        def add_q(i, k):
            part = pl.ds(pl.multiple_of(k * CHUNK, CHUNK), CHUNK)
            for h in range(KEY_VALUE_HEADS):
                q_sum[h] += dotf(scaled[pl.ds(i * HALF, HALF), part], q_w[h, part, :])

        def take_and_add_kv(i, k, carry):
            take_chunk(i, k)
            add_kv(i, k)
            return carry

        def q_only(i, k, carry):
            add_q(i, k)
            return carry

        def chunk(i, k, carry):
            take_chunk(i, k)
            add_kv(i, k)
            add_q(i, k)
            return carry

        kv_weight_copy.wait()
        for i in range(2):
            part, rows = pl.ds(i, 1), pl.ds(i * HALF, HALF)
            kv_sum[...] = jnp.zeros_like(kv_sum)
            q_sum[...] = jnp.zeros_like(q_sum)
            if i == 0:
                lax.fori_loop(0, N_CHUNK, functools.partial(take_and_add_kv, i), 0)
            else:
                lax.fori_loop(0, N_CHUNK - 1, functools.partial(chunk, i), 0)
                take_and_add_kv(i, N_CHUNK - 1, 0)
            inverse = inverse_rms(rows)
            store_kv(i, kv_sum[...], inverse)
            send_kv(part, i, (RELAYED, DIRECT)[i])
            hidden_copy(i).start()
            if i == 0:
                for d in ORDER:
                    q_weight_copy(d).wait()
                lax.fori_loop(0, N_CHUNK, functools.partial(q_only, i), 0)
            else:
                add_q(i, N_CHUNK - 1)
            q_scale = inverse * Q_SCALE
            for d in ORDER:
                h = (a + d) % SIDE
                store_q(h, i, q_sum[h], q_scale)
                if d:
                    q_copy(part, i, d).start()
                else:
                    own_q(part, i).start()
            if i == 0:
                spread(part, i, RELAYED)
        pass_on(pl.ds(0, 1), 0)
        spread(pl.ds(1, 1), 1, DIRECT)
        settle(pl.ds(0, 1), 0, RELAYED)
        settle(pl.ds(1, 1), 1, DIRECT)

    @pl.when(jnp.logical_not(waits))
    def _():
        for i in range(2):
            for k in range(N_CHUNK):
                take_chunk(i, k)
        kv_weight_copy.wait()
        inverse = inverse_rms(pl.ds(0, ROWS))
        sums = dotf(scaled[...], kv_w[...])
        for i in range(2):
            rows = slice(i * HALF, (i + 1) * HALF)
            store_kv(i, sums[rows, :], inverse[rows, :])
        send_kv(everything, 0, RELAYED)
        for i in range(2):
            hidden_copy(i).start()
        q_scale = inverse * Q_SCALE
        for d in ORDER:
            h = (a + d) % SIDE
            q_weight_copy(d).wait()
            group = dotf(scaled[...], q_w[h])
            for i in range(2):
                rows = slice(i * HALF, (i + 1) * HALF)
                store_q(h, i, group[rows, :], q_scale[rows, :])
            if d:
                q_copy(everything, 0, d).start()
            else:
                own_q(everything, 0).start()
        spread(everything, 0, RELAYED)
        pass_on(everything, 0)
        settle(everything, 0, RELAYED)

    for i in range(2):
        hidden_copy(i).wait()

    @pl.when(section < 7)
    def _():
        for i in range(2):
            for k in range(N_CHUNK):
                hand_off(i, k).wait_send()


def exchange(embedded, finished, gain, q_weight, kv_weight):
    hbm = pl.BlockSpec(memory_space=pltpu.HBM)
    vmem = pltpu.VMEM
    dma = pltpu.SemaphoreType.DMA
    return pl.pallas_call(
        exchange_kernel,
        out_shape=(
            jax.ShapeDtypeStruct((SIDE, 2, Q_PART, HEAD_DIM), jnp.bfloat16),
            jax.ShapeDtypeStruct((SIDE, SIDE, 2, KV_PART, HEAD_DIM), jnp.bfloat16),
            jax.ShapeDtypeStruct((ROWS, MODEL), jnp.float32),
        ),
        in_specs=[hbm, hbm, pl.BlockSpec(memory_space=vmem), hbm, hbm],
        out_specs=(hbm, hbm, hbm),
        scratch_shapes=[
            vmem((ROWS, MODEL), jnp.bfloat16),
            vmem((ROWS, MODEL), jnp.float32),
            vmem((ROWS, MODEL), jnp.bfloat16),
            vmem((SIDE, MODEL, HEAD_COLS), jnp.bfloat16),
            vmem((MODEL, 2 * KEY_VALUE_HEADS * HEAD_DIM), jnp.bfloat16),
            vmem((SIDE, HALF, HEAD_COLS), jnp.float32),
            vmem((HALF, 2 * KEY_VALUE_HEADS * HEAD_DIM), jnp.float32),
            vmem((ROWS, QBLOCK), jnp.float32),
            vmem((SIDE, 2, Q_PART, HEAD_DIM), jnp.bfloat16),
            vmem((SIDE, 2, KV_PART, HEAD_DIM), jnp.bfloat16),
            dma((2, N_CHUNK)), dma((2, N_CHUNK)), dma((SIDE + 1,)), dma((2,)), dma((2, 2)),
            dma((2, 3)), dma((2, 3)), dma((2, SIDE, 3)), dma((2, SIDE, 3)),
            dma((2, SIDE)), dma((2, SIDE)), dma((2, 3)), dma((2, 3)),
        ],
        compiler_params=pltpu.CompilerParams(
            collective_id=0, has_side_effects=True, vmem_limit_bytes=60 << 20
        ),
        cost_estimate=pl.CostEstimate(
            flops=2 * ROWS * MODEL * 3584, bytes_accessed=24 << 20, transcendentals=0
        ),
    )(embedded, finished, gain, q_weight, kv_weight)


def attend_kernel(steps, order, q_hbm, kv_hbm, *refs):
    outs = refs[:len(steps)]
    queries, kv, total, peak, slot_of, sems = refs[len(steps):]
    _, _, a, b, stride_a, stride_b = placement()
    kv_copy = pltpu.make_async_copy(kv_hbm, kv, sems.at[0])
    kv_copy.start()
    q_copies = [
        pltpu.make_async_copy(q_hbm.at[e], queries.at[i], sems.at[1 + i]) for i, e in enumerate(steps)
    ]
    for copy in q_copies:
        copy.start()
    for b_of in range(SIDE):
        for a_of in range(SIDE):
            slot_of[order[a_of * stride_a + b_of * stride_b]] = b_of * SIDE + a_of

    kv_copy.wait()
    for copy in q_copies:
        copy.wait()

    ones = jnp.ones((SUM_ROWS, HEAD_DIM), jnp.bfloat16)
    kv_bounds = jnp.max(kv[:, :, 2 * HALF:, :].astype(jnp.float32), axis=(0, 1))
    q_bounds = jnp.max(queries[:, :, GROUP * HALF:, :].astype(jnp.float32), axis=(0, 1))
    small = jnp.logical_and(
        jnp.max(kv_bounds[0:SUM_ROWS // 2, :] * q_bounds[0:SUM_ROWS // 2, :]) <= SCORE_LIMIT * SCORE_LIMIT,
        jnp.max(kv_bounds[SUM_ROWS // 2:, :]) <= VALUE_LIMIT,
    )

    def query_rows(i):
        return jnp.concatenate([queries[i, half, 0:GROUP * HALF, :] for half in range(2)], axis=0)

    def key_rows(slots):
        return jnp.concatenate(
            [kv[slot, half, 0:HALF, :] for slot in slots for half in range(2)], axis=0
        )

    def value_cols(slots):
        parts = [
            jnp.concatenate([kv[slot, half, HALF:2 * HALF, :], ones], axis=0)
            for slot in slots for half in range(2)
        ]
        return jnp.concatenate(parts, axis=1)

    def causal():
        key = lax.broadcasted_iota(jnp.int32, (ROWS, LANES), 0)
        lane = lax.broadcasted_iota(jnp.int32, (ROWS, LANES), 1)
        return key <= lane % HALF + jnp.where(lane >= LANES // 2, HALF, 0)

    def span(i, carry):
        e = steps[0]
        for j in range(1, len(steps)):
            e = jnp.where(i == j, steps[j], e)
        rank = order[((a + e) % SIDE) * stride_a + b * stride_b]

        @pl.when(small)
        def _():
            total[...] = jnp.zeros_like(total)

            def four(c, carry):
                slots = [slot_of[4 * c + j] for j in range(4)]
                weights = jnp.exp2(dotf(key_rows(slots), query_rows(i), NT)).astype(jnp.bfloat16)
                total[...] += dotf(value_cols(slots), weights)
                return carry

            lax.fori_loop(0, rank // 4, four, 0)
            for rest in range(4):

                @pl.when(rank % 4 == rest)
                def _():
                    slots = [slot_of[rank - rest + j] for j in range(rest + 1)]
                    weights = jnp.exp2(dotf(key_rows(slots), query_rows(i), NT))
                    last = jnp.where(causal(), weights[rest * ROWS:, :], 0.0)
                    if rest:
                        last = jnp.concatenate([weights[:rest * ROWS, :], last], axis=0)
                    total[...] += dotf(value_cols(slots), last.astype(jnp.bfloat16))

        @pl.when(jnp.logical_not(small))
        def _():
            total[...] = jnp.zeros_like(total)
            peak[...] = jnp.full_like(peak, MASK_FILLER)

            def one(t, carry):
                slots = [slot_of[t]]
                scores = dotf(key_rows(slots), query_rows(i), NT)
                visible = jnp.logical_or(causal(), t < rank)
                scores = jnp.where(visible, scores, MASK_FILLER)
                before = peak[0:1, :]
                now = jnp.maximum(before, jnp.max(scores, axis=0, keepdims=True))
                weights = jnp.where(visible, jnp.exp2(scores - now), 0.0)
                total[...] = total[...] * jnp.exp2(before - now) + dotf(
                    value_cols(slots), weights.astype(jnp.bfloat16)
                )
                peak[0:1, :] = now
                return carry

            lax.fori_loop(0, rank + 1, one, 0)

        for j in range(len(steps)):

            @pl.when(i == j)
            def _():
                for half in range(2):
                    for g in range(GROUP):
                        first = (half * GROUP + g) * HALF
                        lanes = slice(first, first + HALF)
                        share = total[0:HEAD_DIM, lanes] / total[HEAD_DIM:HEAD_DIM + 1, lanes]
                        rows, cols = slice(half * HALF, (half + 1) * HALF), slice(g * HEAD_DIM, (g + 1) * HEAD_DIM)
                        outs[j][rows, cols] = share.T.astype(jnp.bfloat16)

        return carry

    lax.fori_loop(0, len(steps), span, 0)


def attend(order, q_all, kv_all, steps):
    any_spec = pl.BlockSpec(memory_space=pltpu.HBM)
    vmem = pltpu.VMEM
    out = jax.ShapeDtypeStruct((ROWS, HEAD_COLS), jnp.bfloat16)
    n = len(steps)
    return pl.pallas_call(
        functools.partial(attend_kernel, steps),
        out_shape=(out,) * n,
        in_specs=[pl.BlockSpec(memory_space=pltpu.SMEM), any_spec, any_spec],
        out_specs=(pl.BlockSpec(memory_space=vmem),) * n,
        scratch_shapes=[
            vmem((n, 2, Q_PART, HEAD_DIM), jnp.bfloat16),
            vmem((SIDE * SIDE, 2, KV_PART, HEAD_DIM), jnp.bfloat16),
            vmem((HEAD_DIM + SUM_ROWS, LANES), jnp.float32),
            vmem((8, LANES), jnp.float32),
            pltpu.SMEM((SIDE * SIDE,), jnp.int32),
            pltpu.SemaphoreType.DMA((1 + n,)),
        ],
        compiler_params=pltpu.CompilerParams(vmem_limit_bytes=60 << 20),
        cost_estimate=pl.CostEstimate(
            flops=n * 4 * LANES * HEAD_DIM * 2304, bytes_accessed=3 << 20, transcendentals=n * LANES * 2304
        ),
    )(order, q_all, kv_all.reshape(SIDE * SIDE, 2, KV_PART, HEAD_DIM))


def finish_kernel(p0, p1, p2, p3, hidden, gain, out):
    _, _, a, _, _, _ = placement()
    pieces = [p[...].astype(jnp.float32) for p in (p0, p1, p2, p3)]
    squares = sum(jnp.sum(p * p, axis=1, keepdims=True) for p in pieces)
    inverse = lax.rsqrt(squares * (1.0 / MODEL) + EPSILON)
    for d, piece in enumerate(pieces):
        first = pl.multiple_of(((a + SIDE - d) % SIDE) * HEAD_COLS, HEAD_COLS)
        cols = pl.ds(first, HEAD_COLS)
        rows = hidden[:, cols] + gain[0:1, cols] * (piece * inverse)
        out[:, cols] = rows.astype(jnp.bfloat16)


def finish(pieces, hidden, gain):
    tile = 128
    piece = pl.BlockSpec((tile, HEAD_COLS), lambda i: (i, 0))
    whole = pl.BlockSpec((tile, MODEL), lambda i: (i, 0))
    return pl.pallas_call(
        finish_kernel,
        grid=(ROWS // tile,),
        out_shape=jax.ShapeDtypeStruct((ROWS, MODEL), jnp.bfloat16),
        in_specs=[piece] * 4 + [whole, pl.BlockSpec((1, MODEL), lambda i: (0, 0))],
        out_specs=whole,
        compiler_params=pltpu.CompilerParams(vmem_limit_bytes=60 << 20),
    )(*pieces, hidden, gain)


def send_along(x, d):
    pairs = []
    for section in range(8):
        for ctx in range(16):
            if section % 2:
                to = (ctx + d * SIDE) % 16
            else:
                to = ctx // SIDE * SIDE + (ctx + d) % SIDE
            pairs.append((section * 16 + ctx, section * 16 + to))
    return lax.ppermute(x, ("section", "ctx"), pairs)


def per_device(embedded, finished, norm_gain, q_weight, kv_weight, out_gain, span_order):
    q_all, kv_all, hidden = exchange(
        embedded, finished[0], norm_gain, q_weight[0], kv_weight[0]
    )
    far, near, back = attend(span_order, q_all, kv_all, (2, 1, 3))
    far, near, back = send_along(far, 2), send_along(near, 1), send_along(back, 3)
    (own,) = attend(span_order, q_all, kv_all, (0,))
    return finish((own, near, far, back), hidden, out_gain)[None]


def solution(mesh):
    placed = (
        P("ctx", None),
        P("section", "ctx", None),
        P("section", None),
        P("section", None, None),
        P("section", None, None),
        P("section", None),
        P(),
    )
    return jax.shard_map(
        per_device, mesh=mesh, in_specs=placed, out_specs=P("section", "ctx", None), check_vma=False
    )
```

time: 111 us -> 106 us (0.955)
  the two profiles are of different devices: /device:TPU:106 before, /device:TPU:96 now
where the time goes in v2:
time: 106 us
  Pallas kernels  91.7 us (87%)
  starting transfers between devices  13.4 us (13%)
    pallas_call x2, Pallas kernels, attend(): pl.pallas_call(functools.partial(attend_kernel, steps), out_shape=(out,)...  50.2 us
    pallas_call x1, Pallas kernels, exchange(): pl.pallas_call(exchange_kernel, out_shape=(jax.ShapeDtypeStruct((SIDE, 2,...  37.9 us
    ppermute x3, starting transfers between devices, send_along(): return lax.ppermute(x, ('section', 'ctx'), pairs)  13.4 us
    pallas_call x1, Pallas kernels, finish(): pl.pallas_call(finish_kernel, grid=(ROWS // tile,), out_shape=jax.ShapeDt...  3.53 us
  transfers between devices with their start and end apart: 3, of which 0 were waited for; matrix products, arithmetic and copies ran while one was open for 0% of the time, Pallas kernels for 16%

profile of v2, /device:TPU:96, one launch (start us, length us, event | category | flops | bytes accessed | tf_op | source)
XLA Modules:
  0.0 106.0 jit_solution(11913748884463229834)
XLA Ops:
  0.0 37.9 %shard_map.73 = (bf16[4,2,656,128]{3,2,1,0:T(8,128)(2,1)}, bf16[4,4,2,272,128]{4,3,2,1,0:T(8,128)(2,1)}, f32[256,2560]{1,0:T(8,128)}) custom-call(bf16[256,2560]{1,0:T(8,128)(2,1)} %embedded.1, bf16[256,2560]{1,0:T(8,128)(2,1)} %bitcast.7, f32[1,2560]{1,0:T(1,128)} %gain.2, bf16[2560,2560]{1,0:T(8,128)(2,1)} %bitcast.5, bf16[2560,1024]{1,0:T(8,128)(2,1)} %bitcast.6), custom_call_target="tpu_custom_call" | custom-call | flops 4697620480 | bytes 25165824 | tf_op jit(solution)/shard_map/pallas_call | solution.py:364
  37.9 33.2 %shard_map.75 = (bf16[256,640]{1,0:T(8,128)(2,1)}, bf16[256,640]{1,0:T(8,128)(2,1)}, bf16[256,640]{1,0:T(8,128)(2,1)}) custom-call(s32[16]{0:T(128)} %order.3, bf16[4,2,656,128]{3,2,1,0:T(8,128)(2,1)} %get-tuple-element.11.q_hbm, bf16[16,2,272,128]{3,2,1,0:T(8,128)(2,1)} %bitcast.8), custom_call_target="tpu_custom_call" | custom-call | flops 4529848320 | bytes 3145728 | tf_op jit(solution)/shard_map/pallas_call | solution.py:515
  71.2 10.6 %collective-permute-start = (bf16[256,640]{1,0:T(8,128)(2,1)}, bf16[256,640]{1,0:T(8,128)(2,1)S(1)}, u32[]{:S(2)}, u32[]{:S(2)}) collective-permute-start(bf16[256,640]{1,0:T(8,128)(2,1)} %get-tuple-element.13), channel_id=1, source_target_pairs={{0,1},{1,2},{2,3},{3,0},{4,5},{5,6},{6,7},{7,4},{8,9},{9,10},{10,1... | collective-permute-start | bytes 983048 | tf_op jit(solution)/shard_map/ppermute | solution.py:570
  81.8 0.0 collective-permute-start.1
  81.8 2.8 %collective-permute-start.2 = (bf16[256,640]{1,0:T(8,128)(2,1)}, bf16[256,640]{1,0:T(8,128)(2,1)S(1)}, u32[]{:S(2)}, u32[]{:S(2)}) collective-permute-start(bf16[256,640]{1,0:T(8,128)(2,1)} %get-tuple-element.15), channel_id=1, source_target_pairs={{0,3},{1,0},{2,1},{3,2},{4,7},{5,4},{6,5},{7,6},{8,11},{9,8},{10,9... | collective-permute-start | bytes 983048 | tf_op jit(solution)/shard_map/ppermute | solution.py:570
  84.5 17.0 %shard_map.74.p0 = bf16[256,640]{1,0:T(8,128)(2,1)} custom-call(s32[16]{0:T(128)} %order.3, bf16[4,2,656,128]{3,2,1,0:T(8,128)(2,1)} %get-tuple-element.11.q_hbm, bf16[16,2,272,128]{3,2,1,0:T(8,128)(2,1)} %bitcast.9), custom_call_target="tpu_custom_call" | custom-call | flops 1509949440 | bytes 3145728 | tf_op jit(solution)/shard_map/pallas_call | solution.py:515
  101.5 0.0 collective-permute-done.p1
  101.5 0.0 copy-start
  101.6 0.0 collective-permute-done.1.p2
  101.6 0.0 copy-start.1
  101.6 0.0 collective-permute-done.2.p3
  101.6 0.0 copy-start.2
  101.6 0.7 copy-done
  102.3 0.1 copy-done.1
  102.4 0.1 copy-done.2
  102.5 3.5 %shard_map.76 = bf16[256,2560]{1,0:T(8,128)(2,1)} custom-call(bf16[256,640]{1,0:T(8,128)(2,1)} %shard_map.74.p0, bf16[256,640]{1,0:T(8,128)(2,1)} %copy-done, bf16[256,640]{1,0:T(8,128)(2,1)} %copy-done.1, bf16[256,640]{1,0:T(8,128)(2,1)} %copy-done.2, f32[256,2560]{1,0:T(8,128)} %get-tuple-element.16.hidden, f32[1,2560]{1,0:T(1,128)} %gain.3), custom_call_target="tpu_custom_call" | custom-call | tf_op jit(solution)/shard_map/pallas_call | solution.py:551
Async XLA Ops:
  71.2 30.4 %collective-permute-start = (bf16[256,640]{1,0:T(8,128)(2,1)}, bf16[256,640]{1,0:T(8,128)(2,1)S(1)}, u32[]{:S(2)}, u32[]{:S(2)}) collective-permute-start(bf16[256,640]{1,0:T(8,128)(2,1)} %get-tuple-element.13), channel_id=1, source_target_pairs={{0,1},{1,2},{2,3},{3,0},{4,5},{5,6},{6,7},{7,4},{8,9},{9,10},{10,1... | collective-permute-start | bytes 983048 | tf_op jit(solution)/shard_map/ppermute | solution.py:570
  81.8 19.8 %collective-permute-start.1 = (bf16[256,640]{1,0:T(8,128)(2,1)}, bf16[256,640]{1,0:T(8,128)(2,1)S(1)}, u32[]{:S(2)}, u32[]{:S(2)}) collective-permute-start(bf16[256,640]{1,0:T(8,128)(2,1)} %get-tuple-element.14), channel_id=1, source_target_pairs={{0,2},{1,3},{2,0},{3,1},{4,6},{5,7},{6,4},{7,5},{8,10},{9,11},{10,... | collective-permute-start | bytes 983048 | tf_op jit(solution)/shard_map/ppermute | solution.py:570
  81.8 19.8 %collective-permute-start.2 = (bf16[256,640]{1,0:T(8,128)(2,1)}, bf16[256,640]{1,0:T(8,128)(2,1)S(1)}, u32[]{:S(2)}, u32[]{:S(2)}) collective-permute-start(bf16[256,640]{1,0:T(8,128)(2,1)} %get-tuple-element.15), channel_id=1, source_target_pairs={{0,3},{1,0},{2,1},{3,2},{4,7},{5,4},{6,5},{7,6},{8,11},{9,8},{10,9... | collective-permute-start | bytes 983048 | tf_op jit(solution)/shard_map/ppermute | solution.py:570
  101.5 0.7 copy-start
  101.6 0.8 copy-start.1
  101.6 0.9 copy-start.2

commit v3 on v2

--- a/solution.py
+++ b/solution.py
@@ -394,35 +394,30 @@
     )(embedded, finished, gain, q_weight, kv_weight)
 
 
-def attend_kernel(steps, order, q_hbm, kv_hbm, *refs):
+def attend_kernel(steps, order, q_all, kv, *refs):
     outs = refs[:len(steps)]
-    queries, kv, total, peak, slot_of, sems = refs[len(steps):]
+    total, peak, slot_of = refs[len(steps):]
     _, _, a, b, stride_a, stride_b = placement()
-    kv_copy = pltpu.make_async_copy(kv_hbm, kv, sems.at[0])
-    kv_copy.start()
-    q_copies = [
-        pltpu.make_async_copy(q_hbm.at[e], queries.at[i], sems.at[1 + i]) for i, e in enumerate(steps)
-    ]
-    for copy in q_copies:
-        copy.start()
     for b_of in range(SIDE):
         for a_of in range(SIDE):
             slot_of[order[a_of * stride_a + b_of * stride_b]] = b_of * SIDE + a_of
 
-    kv_copy.wait()
-    for copy in q_copies:
-        copy.wait()
-
     ones = jnp.ones((SUM_ROWS, HEAD_DIM), jnp.bfloat16)
     kv_bounds = jnp.max(kv[:, :, 2 * HALF:, :].astype(jnp.float32), axis=(0, 1))
-    q_bounds = jnp.max(queries[:, :, GROUP * HALF:, :].astype(jnp.float32), axis=(0, 1))
+    q_bounds = jnp.max(q_all[:, :, GROUP * HALF:, :].astype(jnp.float32), axis=(0, 1))
     small = jnp.logical_and(
         jnp.max(kv_bounds[0:SUM_ROWS // 2, :] * q_bounds[0:SUM_ROWS // 2, :]) <= SCORE_LIMIT * SCORE_LIMIT,
         jnp.max(kv_bounds[SUM_ROWS // 2:, :]) <= VALUE_LIMIT,
     )
 
+    def steps_at(i):
+        e = steps[0]
+        for j in range(1, len(steps)):
+            e = jnp.where(i == j, steps[j], e)
+        return e
+
     def query_rows(i):
-        return jnp.concatenate([queries[i, half, 0:GROUP * HALF, :] for half in range(2)], axis=0)
+        return jnp.concatenate([q_all[steps_at(i), half, 0:GROUP * HALF, :] for half in range(2)], axis=0)
 
     def key_rows(slots):
         return jnp.concatenate(
@@ -442,9 +437,7 @@
         return key <= lane % HALF + jnp.where(lane >= LANES // 2, HALF, 0)
 
     def span(i, carry):
-        e = steps[0]
-        for j in range(1, len(steps)):
-            e = jnp.where(i == j, steps[j], e)
+        e = steps_at(i)
         rank = order[((a + e) % SIDE) * stride_a + b * stride_b]
 
         @pl.when(small)
@@ -508,24 +501,20 @@
 
 
 def attend(order, q_all, kv_all, steps):
-    any_spec = pl.BlockSpec(memory_space=pltpu.HBM)
     vmem = pltpu.VMEM
     out = jax.ShapeDtypeStruct((ROWS, HEAD_COLS), jnp.bfloat16)
     n = len(steps)
     return pl.pallas_call(
         functools.partial(attend_kernel, steps),
         out_shape=(out,) * n,
-        in_specs=[pl.BlockSpec(memory_space=pltpu.SMEM), any_spec, any_spec],
+        in_specs=[pl.BlockSpec(memory_space=pltpu.SMEM)] + [pl.BlockSpec(memory_space=vmem)] * 2,
         out_specs=(pl.BlockSpec(memory_space=vmem),) * n,
         scratch_shapes=[
-            vmem((n, 2, Q_PART, HEAD_DIM), jnp.bfloat16),
-            vmem((SIDE * SIDE, 2, KV_PART, HEAD_DIM), jnp.bfloat16),
             vmem((HEAD_DIM + SUM_ROWS, LANES), jnp.float32),
             vmem((8, LANES), jnp.float32),
             pltpu.SMEM((SIDE * SIDE,), jnp.int32),
-            pltpu.SemaphoreType.DMA((1 + n,)),
         ],
-        compiler_params=pltpu.CompilerParams(vmem_limit_bytes=60 << 20),
+        compiler_params=pltpu.CompilerParams(vmem_limit_bytes=24 << 20),
         cost_estimate=pl.CostEstimate(
             flops=n * 4 * LANES * HEAD_DIM * 2304, bytes_accessed=3 << 20, transcendentals=n * LANES * 2304
         ),
@@ -554,7 +543,7 @@
         out_shape=jax.ShapeDtypeStruct((ROWS, MODEL), jnp.bfloat16),
         in_specs=[piece] * 4 + [whole, pl.BlockSpec((1, MODEL), lambda i: (0, 0))],
         out_specs=whole,
-        compiler_params=pltpu.CompilerParams(vmem_limit_bytes=60 << 20),
+        compiler_params=pltpu.CompilerParams(vmem_limit_bytes=16 << 20),
     )(*pieces, hidden, gain)
 
 

time: 106 us -> 93.5 us (0.88)
  the two profiles are of different devices: /device:TPU:96 before, /device:TPU:113 now
where the time goes in v3:
time: 93.5 us; the launch traced here: 93.3 us
  Pallas kernels  74.4 us (80%)
  starting transfers between devices  15.8 us (17%)
  local copies, waits for them, and re-layouts  2.96 us (3%)
    pallas_call x2, Pallas kernels, attend(): pl.pallas_call(functools.partial(attend_kernel, steps), out_shape=(out,)...  38.8 us
    pallas_call x1, Pallas kernels, exchange(): pl.pallas_call(exchange_kernel, out_shape=(jax.ShapeDtypeStruct((SIDE, 2,...  33.9 us
    ppermute x3, starting transfers between devices, send_along(): return lax.ppermute(x, ('section', 'ctx'), pairs)  15.8 us
    unnamed x10, local copies, waits for them, and re-layouts  2.96 us
  transfers between devices with their start and end apart: 3, of which 0 were waited for; matrix products, arithmetic and copies ran while one was open for 0% of the time, Pallas kernels for 15%

profile of v3, /device:TPU:113, one launch (start us, length us, event | category | flops | bytes accessed | tf_op | source)
XLA Modules:
  0.0 93.3 jit_solution(4399364879006402302)
XLA Ops:
  0.0 0.0 copy-start.4
  0.0 33.9 %shard_map.73 = (bf16[4,2,656,128]{3,2,1,0:T(8,128)(2,1)}, bf16[4,4,2,272,128]{4,3,2,1,0:T(8,128)(2,1)}, f32[256,2560]{1,0:T(8,128)}) custom-call(bf16[256,2560]{1,0:T(8,128)(2,1)} %embedded.1, bf16[256,2560]{1,0:T(8,128)(2,1)} %bitcast.9, f32[1,2560]{1,0:T(1,128)} %gain.2, bf16[2560,2560]{1,0:T(8,128)(2,1)} %bitcast.7, bf16[2560,1024]{1,0:T(8,128)(2,1)} %bitcast.8), custom_call_target="tpu_custom_call" | custom-call | flops 4697620480 | bytes 25165824 | tf_op jit(solution)/shard_map/pallas_call | solution.py:364
  33.9 0.0 copy-done.4
  33.9 0.0 copy-start.2
  33.9 1.6 %copy-done.2 = bf16[4,4,2,272,128]{4,3,2,1,0:T(8,128)(2,1)S(1)} copy-done((bf16[4,4,2,272,128]{4,3,2,1,0:T(8,128)(2,1)S(1)}, bf16[4,4,2,272,128]{4,3,2,1,0:T(8,128)(2,1)}, u32[]{:S(2)}) %copy-start.2) | copy-done | bytes 2228248
  35.5 0.0 copy-start.3
  35.5 1.3 %copy-done.3 = bf16[4,2,656,128]{3,2,1,0:T(8,128)(2,1)S(1)} copy-done((bf16[4,2,656,128]{3,2,1,0:T(8,128)(2,1)S(1)}, bf16[4,2,656,128]{3,2,1,0:T(8,128)(2,1)}, u32[]{:S(2)}) %copy-start.3) | copy-done | bytes 1343512
  36.8 24.3 %shard_map.75 = (bf16[256,640]{1,0:T(8,128)(2,1)S(1)}, bf16[256,640]{1,0:T(8,128)(2,1)S(1)}, bf16[256,640]{1,0:T(8,128)(2,1)S(1)}) custom-call(s32[16]{0:T(128)S(1)} %copy-done.4, bf16[4,2,656,128]{3,2,1,0:T(8,128)(2,1)S(1)} %copy-done.3, bf16[16,2,272,128]{3,2,1,0:T(8,128)(2,1)S(1)} %bitcast.5), custom_call_target="tpu_custom_call" | custom-call | flops 4529848320 | bytes 3145728 | tf_op jit(solution)/shard_map/pallas_call | solution.py:507
  61.2 2.1 %collective-permute-start = (bf16[256,640]{1,0:T(8,128)(2,1)S(1)}, bf16[256,640]{1,0:T(8,128)(2,1)S(1)}, u32[]{:S(2)}, u32[]{:S(2)}) collective-permute-start(bf16[256,640]{1,0:T(8,128)(2,1)S(1)} %get-tuple-element.13), channel_id=1, source_target_pairs={{0,1},{1,2},{2,3},{3,0},{4,5},{5,6},{6,7},{7,4},{8,9},{9,10},{10,1... | collective-permute-start | bytes 983048 | tf_op jit(solution)/shard_map/ppermute | solution.py:559
  63.2 11.8 %collective-permute-start.1 = (bf16[256,640]{1,0:T(8,128)(2,1)S(1)}, bf16[256,640]{1,0:T(8,128)(2,1)S(1)}, u32[]{:S(2)}, u32[]{:S(2)}) collective-permute-start(bf16[256,640]{1,0:T(8,128)(2,1)S(1)} %get-tuple-element.14), channel_id=1, source_target_pairs={{0,2},{1,3},{2,0},{3,1},{4,6},{5,7},{6,4},{7,5},{8,10},{9,11},{10,... | collective-permute-start | bytes 983048 | tf_op jit(solution)/shard_map/ppermute | solution.py:559
  75.0 0.0 copy-start
  75.0 0.0 copy-start.1
  75.0 2.0 %collective-permute-start.2 = (bf16[256,640]{1,0:T(8,128)(2,1)S(1)}, bf16[256,640]{1,0:T(8,128)(2,1)S(1)}, u32[]{:S(2)}, u32[]{:S(2)}) collective-permute-start(bf16[256,640]{1,0:T(8,128)(2,1)S(1)} %get-tuple-element.15), channel_id=1, source_target_pairs={{0,3},{1,0},{2,1},{3,2},{4,7},{5,4},{6,5},{7,6},{8,11},{9,8},{10,9... | collective-permute-start | bytes 983048 | tf_op jit(solution)/shard_map/ppermute | solution.py:559
  77.0 14.5 %shard_map.74.p0 = bf16[256,640]{1,0:T(8,128)(2,1)S(1)} custom-call(s32[16]{0:T(128)S(1)} %copy-done.4, bf16[4,2,656,128]{3,2,1,0:T(8,128)(2,1)S(1)} %copy-done.3, bf16[16,2,272,128]{3,2,1,0:T(8,128)(2,1)S(1)} %bitcast.6), custom_call_target="tpu_custom_call" | custom-call | flops 1509949440 | bytes 3145728 | tf_op jit(solution)/shard_map/pallas_call | solution.py:507
  91.5 0.0 collective-permute-done.p1
  91.5 0.0 collective-permute-done.1.p2
  91.5 0.0 collective-permute-done.2.p3
  91.5 0.0 copy-done
  91.5 0.0 copy-done.1
  91.5 1.7 %shard_map.76 = bf16[256,2560]{1,0:T(8,128)(2,1)} custom-call(bf16[256,640]{1,0:T(8,128)(2,1)S(1)} %shard_map.74.p0, bf16[256,640]{1,0:T(8,128)(2,1)S(1)} %collective-permute-done.p1, bf16[256,640]{1,0:T(8,128)(2,1)S(1)} %collective-permute-done.1.p2, bf16[256,640]{1,0:T(8,128)(2,1)S(1)} %collective-permute-done.2.p3, f32[256,2560]{1,0:T(8,128)S(1)} %copy-done, ...), custom_call_target="tpu_custom_call" | custom-call | tf_op jit(solution)/shard_map/pallas_call | solution.py:540
Async XLA Ops:
  0.0 33.9 %copy-start.4 = (s32[16]{0:T(128)S(1)}, s32[16]{0:T(128)}, u32[]{:S(2)}) copy-start(s32[16]{0:T(128)} %order.3) | copy-start | bytes 196
  33.9 1.6 %copy-start.2 = (bf16[4,4,2,272,128]{4,3,2,1,0:T(8,128)(2,1)S(1)}, bf16[4,4,2,272,128]{4,3,2,1,0:T(8,128)(2,1)}, u32[]{:S(2)}) copy-start(bf16[4,4,2,272,128]{4,3,2,1,0:T(8,128)(2,1)} %get-tuple-element.12) | copy-start | bytes 6684676
  35.5 1.3 %copy-start.3 = (bf16[4,2,656,128]{3,2,1,0:T(8,128)(2,1)S(1)}, bf16[4,2,656,128]{3,2,1,0:T(8,128)(2,1)}, u32[]{:S(2)}) copy-start(bf16[4,2,656,128]{3,2,1,0:T(8,128)(2,1)} %get-tuple-element.11.q_all) | copy-start | bytes 4030468
  61.2 30.3 %collective-permute-start = (bf16[256,640]{1,0:T(8,128)(2,1)S(1)}, bf16[256,640]{1,0:T(8,128)(2,1)S(1)}, u32[]{:S(2)}, u32[]{:S(2)}) collective-permute-start(bf16[256,640]{1,0:T(8,128)(2,1)S(1)} %get-tuple-element.13), channel_id=1, source_target_pairs={{0,1},{1,2},{2,3},{3,0},{4,5},{5,6},{6,7},{7,4},{8,9},{9,10},{10,1... | collective-permute-start | bytes 983048 | tf_op jit(solution)/shard_map/ppermute | solution.py:559
  63.2 28.3 %collective-permute-start.1 = (bf16[256,640]{1,0:T(8,128)(2,1)S(1)}, bf16[256,640]{1,0:T(8,128)(2,1)S(1)}, u32[]{:S(2)}, u32[]{:S(2)}) collective-permute-start(bf16[256,640]{1,0:T(8,128)(2,1)S(1)} %get-tuple-element.14), channel_id=1, source_target_pairs={{0,2},{1,3},{2,0},{3,1},{4,6},{5,7},{6,4},{7,5},{8,10},{9,11},{10,... | collective-permute-start | bytes 983048 | tf_op jit(solution)/shard_map/ppermute | solution.py:559
  75.0 16.5 %copy-start = (f32[256,2560]{1,0:T(8,128)S(1)}, f32[256,2560]{1,0:T(8,128)}, u32[]{:S(2)}) copy-start(f32[256,2560]{1,0:T(8,128)} %get-tuple-element.16.hidden) | copy-start | bytes 7864324
  75.0 16.5 %copy-start.1 = (f32[1,2560]{1,0:T(1,128)S(1)}, f32[1,2560]{1,0:T(1,128)}, u32[]{:S(2)}) copy-start(f32[1,2560]{1,0:T(1,128)} %gain.3) | copy-start | bytes 30724
  75.0 16.5 %collective-permute-start.2 = (bf16[256,640]{1,0:T(8,128)(2,1)S(1)}, bf16[256,640]{1,0:T(8,128)(2,1)S(1)}, u32[]{:S(2)}, u32[]{:S(2)}) collective-permute-start(bf16[256,640]{1,0:T(8,128)(2,1)S(1)} %get-tuple-element.15), channel_id=1, source_target_pairs={{0,3},{1,0},{2,1},{3,2},{4,7},{5,4},{6,5},{7,6},{8,11},{9,8},{10,9... | collective-permute-start | bytes 983048 | tf_op jit(solution)/shard_map/ppermute | solution.py:559

commit v4 on v3

--- a/solution.py
+++ b/solution.py
@@ -241,8 +241,8 @@
         own_kv(part, i).wait()
         own_q(part, i).wait()
         for d in range(1, SIDE):
+            kv_copy(part, i, d).wait_send()
             q_copy(part, i, d).wait()
-            kv_copy(part, i, d).wait_send()
         for p in range(SIDE):
             if len(ways) == 3:
                 for way in ways:
@@ -252,6 +252,16 @@
                 for way in ways:
                     row_copy(part, i, p, way).wait_send()
                 on_copy(part, i, p).wait()
+
+    def leave():
+        for i in range(2):
+            hidden_copy(i).wait()
+
+        @pl.when(section < 7)
+        def _():
+            for i in range(2):
+                for k in range(N_CHUNK):
+                    hand_off(i, k).wait_send()
 
     square_sum[...] = jnp.zeros_like(square_sum)
     waits = jnp.logical_and(section % 2 == 0, section > 0)
@@ -314,6 +324,7 @@
                 spread(part, i, RELAYED)
         pass_on(pl.ds(0, 1), 0)
         spread(pl.ds(1, 1), 1, DIRECT)
+        leave()
         settle(pl.ds(0, 1), 0, RELAYED)
         settle(pl.ds(1, 1), 1, DIRECT)
 
@@ -345,16 +356,8 @@
                 own_q(everything, 0).start()
         spread(everything, 0, RELAYED)
         pass_on(everything, 0)
+        leave()
         settle(everything, 0, RELAYED)
-
-    for i in range(2):
-        hidden_copy(i).wait()
-
-    @pl.when(section < 7)
-    def _():
-        for i in range(2):
-            for k in range(N_CHUNK):
-                hand_off(i, k).wait_send()
 
 
 def exchange(embedded, finished, gain, q_weight, kv_weight):
@@ -386,7 +389,7 @@
             dma((2, SIDE)), dma((2, SIDE)), dma((2, 3)), dma((2, 3)),
         ],
         compiler_params=pltpu.CompilerParams(
-            collective_id=0, has_side_effects=True, vmem_limit_bytes=60 << 20
+            collective_id=0, has_side_effects=True, vmem_limit_bytes=44 << 20
         ),
         cost_estimate=pl.CostEstimate(
             flops=2 * ROWS * MODEL * 3584, bytes_accessed=24 << 20, transcendentals=0
@@ -444,13 +447,18 @@
         def _():
             total[...] = jnp.zeros_like(total)
 
-            def four(c, carry):
-                slots = [slot_of[4 * c + j] for j in range(4)]
+            def blocks(count, c, carry):
+                slots = [slot_of[count * c + j] for j in range(count)]
                 weights = jnp.exp2(dotf(key_rows(slots), query_rows(i), NT)).astype(jnp.bfloat16)
                 total[...] += dotf(value_cols(slots), weights)
                 return carry
 
-            lax.fori_loop(0, rank // 4, four, 0)
+            lax.fori_loop(0, rank // 8, functools.partial(blocks, 8), 0)
+
+            @pl.when(rank % 8 >= 4)
+            def _():
+                blocks(4, 2 * (rank // 8), 0)
+
             for rest in range(4):
 
                 @pl.when(rank % 4 == rest)

time: 93.5 us -> 90.8 us (0.971)
  the two profiles are of different devices: /device:TPU:113 before, /device:TPU:110 now
where the time goes in v4:
time: 90.8 us; the launch traced here: 90.6 us
  Pallas kernels  72.6 us (80%)
  starting transfers between devices  14.6 us (16%)
  local copies, waits for them, and re-layouts  3.34 us (4%)
    pallas_call x2, Pallas kernels, attend(): pl.pallas_call(functools.partial(attend_kernel, steps), out_shape=(out,)...  36.3 us
    pallas_call x1, Pallas kernels, exchange(): pl.pallas_call(exchange_kernel, out_shape=(jax.ShapeDtypeStruct((SIDE, 2,...  34.5 us
    ppermute x3, starting transfers between devices, send_along(): return lax.ppermute(x, ('section', 'ctx'), pairs)  14.6 us
    unnamed x10, local copies, waits for them, and re-layouts  3.34 us
  transfers between devices with their start and end apart: 3, of which 0 were waited for; matrix products, arithmetic and copies ran while one was open for 0% of the time, Pallas kernels for 16%

profile of v4, /device:TPU:110, one launch (start us, length us, event | category | flops | bytes accessed | tf_op | source)
XLA Modules:
  0.0 90.6 jit_solution(11528937839131651115)
XLA Ops:
  0.0 0.0 copy-start
  0.0 1.3 %copy-done = bf16[256,2560]{1,0:T(8,128)(2,1)S(1)} copy-done((bf16[256,2560]{1,0:T(8,128)(2,1)S(1)}, bf16[256,2560]{1,0:T(8,128)(2,1)}, u32[]{:S(2)}) %copy-start) | copy-done | bytes 1310744
  1.3 0.0 copy-start.1
  1.3 1.3 %copy-done.1 = bf16[1,256,2560]{2,1,0:T(8,128)(2,1)S(1)} copy-done((bf16[1,256,2560]{2,1,0:T(8,128)(2,1)S(1)}, bf16[1,256,2560]{2,1,0:T(8,128)(2,1)}, u32[]{:S(2)}) %copy-start.1) | copy-done | bytes 1310744
  2.6 0.0 copy-start.2
  2.6 0.7 copy-done.2
  3.3 0.0 copy-start.4
  3.3 34.5 %shard_map.73 = (bf16[4,2,656,128]{3,2,1,0:T(8,128)(2,1)S(1)}, bf16[4,4,2,272,128]{4,3,2,1,0:T(8,128)(2,1)S(1)}, f32[256,2560]{1,0:T(8,128)S(1)}) custom-call(bf16[256,2560]{1,0:T(8,128)(2,1)S(1)} %copy-done, bf16[256,2560]{1,0:T(8,128)(2,1)S(1)} %bitcast.5, f32[1,2560]{1,0:T(1,128)S(1)} %copy-done.2, bf16[2560,2560]{1,0:T(8,128)(2,1)} %bitcast.8, ...), custom_call_target="tpu_custom_call" | custom-call | flops 4697620480 | bytes 25165824 | tf_op jit(solution)/shard_map/pallas_call | solution.py:367
  37.9 0.0 copy-done.4
  37.9 21.8 %shard_map.75 = (bf16[256,640]{1,0:T(8,128)(2,1)S(1)}, bf16[256,640]{1,0:T(8,128)(2,1)S(1)}, bf16[256,640]{1,0:T(8,128)(2,1)S(1)}) custom-call(s32[16]{0:T(128)S(1)} %copy-done.4, bf16[4,2,656,128]{3,2,1,0:T(8,128)(2,1)S(1)} %get-tuple-element.11.q_all, bf16[16,2,272,128]{3,2,1,0:T(8,128)(2,1)S(1)} %bitcast.6), custom_call_target="tpu_custom_call" | custom-call | flops 4529848320 | bytes 3145728 | tf_op jit(solution)/shard_map/pallas_call | solution.py:515
  59.7 8.0 %collective-permute-start = (bf16[256,640]{1,0:T(8,128)(2,1)S(1)}, bf16[256,640]{1,0:T(8,128)(2,1)S(1)}, u32[]{:S(2)}, u32[]{:S(2)}) collective-permute-start(bf16[256,640]{1,0:T(8,128)(2,1)S(1)} %get-tuple-element.13), channel_id=1, source_target_pairs={{0,1},{1,2},{2,3},{3,0},{4,5},{5,6},{6,7},{7,4},{8,9},{9,10},{10,1... | collective-permute-start | bytes 983048 | tf_op jit(solution)/shard_map/ppermute | solution.py:567
  67.7 4.1 %collective-permute-start.1 = (bf16[256,640]{1,0:T(8,128)(2,1)S(1)}, bf16[256,640]{1,0:T(8,128)(2,1)S(1)}, u32[]{:S(2)}, u32[]{:S(2)}) collective-permute-start(bf16[256,640]{1,0:T(8,128)(2,1)S(1)} %get-tuple-element.14), channel_id=1, source_target_pairs={{0,2},{1,3},{2,0},{3,1},{4,6},{5,7},{6,4},{7,5},{8,10},{9,11},{10,... | collective-permute-start | bytes 983048 | tf_op jit(solution)/shard_map/ppermute | solution.py:567
  71.8 0.0 copy-start.3
  71.8 2.5 %collective-permute-start.2 = (bf16[256,640]{1,0:T(8,128)(2,1)S(1)}, bf16[256,640]{1,0:T(8,128)(2,1)S(1)}, u32[]{:S(2)}, u32[]{:S(2)}) collective-permute-start(bf16[256,640]{1,0:T(8,128)(2,1)S(1)} %get-tuple-element.15), channel_id=1, source_target_pairs={{0,3},{1,0},{2,1},{3,2},{4,7},{5,4},{6,5},{7,6},{8,11},{9,8},{10,9... | collective-permute-start | bytes 983048 | tf_op jit(solution)/shard_map/ppermute | solution.py:567
  74.3 14.5 %shard_map.74.p0 = bf16[256,640]{1,0:T(8,128)(2,1)S(1)} custom-call(s32[16]{0:T(128)S(1)} %copy-done.4, bf16[4,2,656,128]{3,2,1,0:T(8,128)(2,1)S(1)} %get-tuple-element.11.q_all, bf16[16,2,272,128]{3,2,1,0:T(8,128)(2,1)S(1)} %bitcast.7), custom_call_target="tpu_custom_call" | custom-call | flops 1509949440 | bytes 3145728 | tf_op jit(solution)/shard_map/pallas_call | solution.py:515
  88.9 0.0 collective-permute-done.p1
  88.9 0.0 collective-permute-done.1.p2
  88.9 0.0 collective-permute-done.2.p3
  88.9 0.0 copy-done.3
  88.9 1.7 %shard_map.76 = bf16[256,2560]{1,0:T(8,128)(2,1)} custom-call(bf16[256,640]{1,0:T(8,128)(2,1)S(1)} %shard_map.74.p0, bf16[256,640]{1,0:T(8,128)(2,1)S(1)} %collective-permute-done.p1, bf16[256,640]{1,0:T(8,128)(2,1)S(1)} %collective-permute-done.1.p2, bf16[256,640]{1,0:T(8,128)(2,1)S(1)} %collective-permute-done.2.p3, ...), custom_call_target="tpu_custom_call" | custom-call | tf_op jit(solution)/shard_map/pallas_call | solution.py:548
Async XLA Ops:
  0.0 1.3 %copy-start = (bf16[256,2560]{1,0:T(8,128)(2,1)S(1)}, bf16[256,2560]{1,0:T(8,128)(2,1)}, u32[]{:S(2)}) copy-start(bf16[256,2560]{1,0:T(8,128)(2,1)} %embedded.1) | copy-start | bytes 3932164
  1.3 1.3 %copy-start.1 = (bf16[1,256,2560]{2,1,0:T(8,128)(2,1)S(1)}, bf16[1,256,2560]{2,1,0:T(8,128)(2,1)}, u32[]{:S(2)}) copy-start(bf16[1,256,2560]{2,1,0:T(8,128)(2,1)} %param.8) | copy-start | bytes 3932164
  2.6 0.7 copy-start.2
  3.3 34.6 %copy-start.4 = (s32[16]{0:T(128)S(1)}, s32[16]{0:T(128)}, u32[]{:S(2)}) copy-start(s32[16]{0:T(128)} %order.3) | copy-start | bytes 196
  59.7 29.1 %collective-permute-start = (bf16[256,640]{1,0:T(8,128)(2,1)S(1)}, bf16[256,640]{1,0:T(8,128)(2,1)S(1)}, u32[]{:S(2)}, u32[]{:S(2)}) collective-permute-start(bf16[256,640]{1,0:T(8,128)(2,1)S(1)} %get-tuple-element.13), channel_id=1, source_target_pairs={{0,1},{1,2},{2,3},{3,0},{4,5},{5,6},{6,7},{7,4},{8,9},{9,10},{10,1... | collective-permute-start | bytes 983048 | tf_op jit(solution)/shard_map/ppermute | solution.py:567
  67.7 21.2 %collective-permute-start.1 = (bf16[256,640]{1,0:T(8,128)(2,1)S(1)}, bf16[256,640]{1,0:T(8,128)(2,1)S(1)}, u32[]{:S(2)}, u32[]{:S(2)}) collective-permute-start(bf16[256,640]{1,0:T(8,128)(2,1)S(1)} %get-tuple-element.14), channel_id=1, source_target_pairs={{0,2},{1,3},{2,0},{3,1},{4,6},{5,7},{6,4},{7,5},{8,10},{9,11},{10,... | collective-permute-start | bytes 983048 | tf_op jit(solution)/shard_map/ppermute | solution.py:567
  71.8 17.1 %copy-start.3 = (f32[1,2560]{1,0:T(1,128)S(1)}, f32[1,2560]{1,0:T(1,128)}, u32[]{:S(2)}) copy-start(f32[1,2560]{1,0:T(1,128)} %gain.3) | copy-start | bytes 30724
  71.8 17.1 %collective-permute-start.2 = (bf16[256,640]{1,0:T(8,128)(2,1)S(1)}, bf16[256,640]{1,0:T(8,128)(2,1)S(1)}, u32[]{:S(2)}, u32[]{:S(2)}) collective-permute-start(bf16[256,640]{1,0:T(8,128)(2,1)S(1)} %get-tuple-element.15), channel_id=1, source_target_pairs={{0,3},{1,0},{2,1},{3,2},{4,7},{5,4},{6,5},{7,6},{8,11},{9,8},{10,9... | collective-permute-start | bytes 983048 | tf_op jit(solution)/shard_map/ppermute | solution.py:567
